TPU v7x, 256 devices: a whole 4x4x8 slice. The times are simulated.
256 devices in a mesh: dp: 16 (over z_lo, x, core), layer: 16 (over z_hi, y).
Axes of the slice: x: 4, y: 4, z: 8 (z_hi: 4, z_lo: 2; z = z_hi * 2 + z_lo), core: 2. Of those that a mesh axis runs over, the one named last changes fastest.
Arguments:
- query_grads: bfloat16 [256, 2, 16, 4096], P(('dp', 'layer')), may hold values from -6 to 6
- corpus_grads: bfloat16 [24576, 16, 4096], P('dp', 'layer'), may hold values from -240 to 240
- left_inverse: float32 [16, 64, 64], P('layer'), may hold values from -2.5 to 2.5
- right_inverse: float32 [16, 64, 64], P('layer'), may hold values from -2.5 to 2.5
Outputs:
- scores: float32 [256, 2, 24576], P('layer', None, 'dp')
All inputs are finite; a program needn't handle non-finite values.
Results may differ from a plain program's by a relative error of at most 0.0029.
Values may be sent and summed in bfloat16 or wider, within the bound.
No kernel may reach another device: no remote copies, remote signals or barrier semaphores. Data moves between devices by JAX's collectives and lax.ppermute only.
A program may use at most 128 MiB of HBM per device.

v0:
```python
import jax
import jax.numpy as jnp
from jax import lax
from jax.sharding import PartitionSpec as P


def precondition(raw, left, right):
    rows, groups, count, width = raw.shape
    din = left.shape[1]
    dout = right.shape[1]
    values = raw.astype(jnp.float32).reshape(rows, groups, count, din, dout)
    result = jnp.einsum(
        "lai,rblij,ljc->rblac", left, values, right, precision=lax.Precision.HIGHEST
    )
    return result.reshape(rows, groups, count, din * dout).astype(jnp.bfloat16)


def per_device(query_grads, corpus_grads, left_inverse, right_inverse):
    groups = query_grads.shape[1]
    width = query_grads.shape[3]
    local_layers = corpus_grads.shape[1]
    examples = corpus_grads.shape[0]
    owned = lax.all_to_all(query_grads, "layer", split_axis=2, concat_axis=0, tiled=True)
    ready = lax.all_gather(
        precondition(owned, left_inverse, right_inverse), "dp", axis=0, tiled=True
    )
    share = ready.shape[0] // lax.axis_size("layer")
    flat = ready[:, :, 0, :].reshape(share * lax.axis_size("layer") * groups, width)
    total = lax.dot_general(
        flat, corpus_grads[:, 0, :], (((1,), (1,)), ((), ())), preferred_element_type=jnp.float32
    )
    totals = lax.psum_scatter(
        total.reshape(share * lax.axis_size("layer"), groups, examples),
        "layer",
        scatter_dimension=0,
        tiled=True,
    )
    wide = corpus_grads.astype(jnp.float32)
    power = lax.psum(jnp.sum(wide * wide, axis=(1, 2)), "layer")
    entries = local_layers * lax.axis_size("layer") * width
    factor = lax.rsqrt(power / entries + 1e-06)
    return totals * factor[None, None, :]


def solution(mesh):
    return jax.shard_map(
        per_device,
        mesh=mesh,
        in_specs=(
            P(("dp", "layer"), None, None, None),
            P("dp", "layer", None),
            P("layer", None, None),
            P("layer", None, None),
        ),
        out_specs=P("layer", None, "dp"),
        check_vma=False,
    )
```

profile of v0, /device:TPU:24, one launch (start us, length us, event | category | flops | bytes accessed | tf_op | source)
XLA Modules:
  0.0 182.6 jit_solution(12013101197607562006)
XLA Ops:
  6.5 0.0 copy-start
  6.5 0.0 all-gather.2.cloned.1.call-start
  6.5 1.2 copy.7
  7.8 21.8 %all_to_all.15 = bf16[1,2,16,4096]{3,1,0,2:T(2,128)(2,1)S(1)} all-to-all(bf16[1,2,16,4096]{3,1,0,2:T(2,128)(2,1)S(1)} %copy.7), channel_id=1, replica_groups=mesh['dp'=16,'layer'=16] {'layer'}, dimensions={2} | all-to-all | bytes 524288 | tf_op jit(solution)/shard_map/all_to_all | solution.py:23
  29.5 0.3 reshape.35
  29.9 0.0 copy-done
  29.9 0.6 fusion.4
  30.5 1.7 convolution_convert_fusion
  32.2 0.4 convert_element_type.19
  32.6 0.8 copy.8
  33.4 0.0 all-gather.2.cloned.1.call-update
  33.5 0.0 reduce-scatter.2.cloned.1.call-start
  33.5 37.5 %all-gather.2.cloned.1.call-done = bf16[256,2,1,4096]{3,0,1,2:T(8,128)(2,1)} async-done(((bf16[16,2,1,4096]{3,0,1,2:T(8,128)(2,1)}), bf16[256,2,1,4096]{3,0,1,2:T(8,128)(2,1)}) %all-gather.2.cloned.1.call-update) | async-done | bytes 4194320 | tf_op jit(solution)/shard_map/all_gather | solution.py:24
  71.0 12.2 %fusion = f32[256,2,1536]{2,0,1:T(8,128)} fusion(bf16[1536,1,4096]{2,0,1:T(8,128)(2,1)} %param.5, bf16[256,2,1,4096]{3,0,1,2:T(8,128)(2,1)} %all-gather.2.cloned.1.call-done), kind=kOutput, calls=%fused_computation.1 | convolution fusion | flops 6442450944 | bytes 19922944 | tf_op jit(solution)/shard_map/dot_general | solution.py:29
  83.2 0.0 reduce-scatter.2.cloned.1.call-update
  83.2 7.1 %multiply_reduce_fusion = f32[1536]{0:T(1024)S(1)} fusion(bf16[1536,1,4096]{2,0,1:T(8,128)(2,1)} %param.5), kind=kLoop, calls=%fused_computation | loop fusion | flops 18872832 | bytes 12589056 | tf_op jit(solution)/shard_map/reduce_sum | solution.py:39
  90.3 35.8 %psum.7 = f32[1536]{0:T(1024)S(1)} all-reduce(f32[1536]{0:T(1024)S(1)} %multiply_reduce_fusion), channel_id=1, replica_groups=mesh['dp'=16,'layer'=16] {'layer'}, use_global_device_ids=true, to_apply=%region_2.0 | all-reduce | flops 1536 | bytes 12288 | tf_op jit(solution)/shard_map/psum | solution.py:39
  126.1 47.8 %reduce-scatter.2.cloned.1.call-done = f32[16,2,1536]{2,0,1:T(8,128)} async-done(((f32[256,2,1536]{2,0,1:T(8,128)}), f32[16,2,1536]{2,0,1:T(8,128)}) %reduce-scatter.2.cloned.1.call-update) | async-done | bytes 196624 | tf_op jit(solution)/shard_map/reduce_scatter | solution.py:32
  174.0 0.9 broadcast_multiply_fusion
  174.9 0.8 copy.9
  (1 shorter events, 0.0 us)
Async XLA Ops:
  6.5 23.4 %copy-start = (f32[1,64,64]{2,1,0:T(8,128)S(1)}, f32[1,64,64]{2,1,0:T(8,128)}, u32[]{:S(2)}) copy-start(f32[1,64,64]{2,1,0:T(8,128)} %param.6) | copy-start | bytes 49156
  6.5 64.5 %all-gather.2.cloned.1.call-start = ((), (), s32[]{:S(2)}) async-start(), calls=%async_computation.2 | async-start | bytes 4456448 | tf_op jit(solution)/shard_map/all_gather | solution.py:24
  33.5 140.5 %reduce-scatter.2.cloned.1.call-start = ((), (), s32[]{:S(2)}) async-start(), calls=%async_computation.3 | async-start | bytes 3342336 | tf_op jit(solution)/shard_map/reduce_scatter | solution.py:32
Sparse Core Ops, SparseCore 0:
  33.6 37.3 all-gather.1
  83.3 90.5 reduce-scatter.1
where the time goes:
time: 184 us; the launch traced here: 183 us
  waiting for transfers between devices  85.3 us (46%)
  blocking collectives  57.6 us (31%)
  matrix products  14.5 us (8%)
  between operations  13.5 us (7%)
  other arithmetic  8.02 us (4%)
  local copies, waits for them, and re-layouts  3.65 us (2%)
    reduce_scatter x1, waiting for transfers between devices, per_device(): lax.psum_scatter(total.reshape(share * lax.axis_size('layer'), groups, ex...  47.8 us
    all_gather x1, waiting for transfers between devices, per_device(): lax.all_gather(precondition(owned, left_inverse, right_inverse), 'dp', ax...  37.5 us
    psum x1, blocking collectives, per_device(): power = lax.psum(jnp.sum(wide * wide, axis=(1, 2)), 'layer')  35.8 us
    all_to_all x1, blocking collectives, per_device(): lax.all_to_all(query_grads, 'layer', split_axis=2, concat_axis=0, tiled=T...  21.8 us
    dot_general x1, matrix products, per_device(): lax.dot_general(flat, corpus_grads[:, 0, :], (((1,), (1,)), ((), ())), pr...  12.2 us
    reduce_sum x1, other arithmetic, per_device(): power = lax.psum(jnp.sum(wide * wide, axis=(1, 2)), 'layer')  7.07 us
  transfers between devices with their start and end apart: 2, of which 2 were waited for; matrix products, arithmetic and copies ran while one was open for 4% of the time, Pallas kernels for 0%

commit v1 on v0

v1 whole, which is shorter than its diff:
```python
import functools

import jax
import jax.numpy as jnp
from jax import lax
from jax.experimental import pallas as pl
from jax.experimental.pallas import tpu as pltpu
from jax.sharding import PartitionSpec as P

F32, BF16 = jnp.float32, jnp.bfloat16
SIZES = {"zl": 2, "x": 4, "c": 2, "zh": 4, "y": 4}
ROWS, WIDTH, LAYERS = 32, 4096, 16
VMEM_LIMIT = 56 * 1024 * 1024


def whole(*shape):
    return pl.BlockSpec(shape, lambda *_: (0,) * len(shape))


def any_space():
    return pl.BlockSpec(memory_space=pl.ANY)


def shifted(value, **shift):
    pairs = []
    for index in range(256):
        dp, layer = divmod(index, 16)
        at = {"zl": dp // 8, "x": dp // 2 % 4, "c": dp % 2, "zh": layer // 4, "y": layer % 4}
        for name, by in shift.items():
            at[name] = (at[name] + by) % SIZES[name]
        pairs.append((index, (at["zl"] * 8 + at["x"] * 2 + at["c"]) * 16 + at["zh"] * 4 + at["y"]))
    return lax.ppermute(value, ("dp", "layer"), pairs)


def pack_kernel(x_ref, out_ref, scratch):
    for b in range(2):
        for r in range(32):
            piece = x_ref[b, :, r * 128 : (r + 1) * 128].astype(F32)
            scratch[pl.ds(b * 32 + r, LAYERS, stride=64), :] = piece
    out_ref[...] = scratch[...].astype(BF16).reshape(LAYERS, 64, 128)


def pack(x):
    return pl.pallas_call(
        pack_kernel,
        out_shape=jax.ShapeDtypeStruct((LAYERS, 64, 128), BF16),
        scratch_shapes=[pltpu.VMEM((LAYERS * 64, 128), F32)],
        compiler_params=pltpu.CompilerParams(vmem_limit_bytes=VMEM_LIMIT),
        cost_estimate=pl.CostEstimate(flops=0, bytes_accessed=524288, transcendentals=0),
        name="pack",
    )(x)


def ready_kernel(x_ref, left_ref, right_ref, out_ref, scratch):
    right = right_ref[...]
    x = x_ref[...].reshape(16 * 64, 128).astype(F32)
    y = jnp.dot(x, right, precision=lax.Precision.HIGHEST, preferred_element_type=F32)
    wide = jnp.concatenate([y[i * 32 : (i + 1) * 32] for i in range(32)], axis=1)
    z = jnp.dot(left_ref[...], wide, precision=lax.Precision.HIGHEST, preferred_element_type=F32)
    low = lax.broadcasted_iota(jnp.int32, (32, 128), 1) < 64
    for i in range(32):
        part = z[:, i * 128 : (i + 1) * 128]
        even, odd = part[0:32], part[32:64]
        even2, odd2 = part[64:96], part[96:128]
        first = even + pltpu.roll(odd, 64, 1)
        second = pltpu.roll(even2, 64, 1) + odd2
        scratch[i * 32 : (i + 1) * 32, :] = jnp.where(low, first, second)
    for r in range(32):
        out_ref[:, r * 128 : (r + 1) * 128] = scratch[pl.ds(r, 32, stride=32), :].astype(BF16)


def make_ready(x, left, right):
    zero = jnp.zeros_like(right)
    diagonal = jnp.concatenate(
        [jnp.concatenate([right, zero], 1), jnp.concatenate([zero, right], 1)], 0
    )
    spread = left.reshape(32, 2, 32, 2).transpose(1, 3, 0, 2).reshape(128, 32)
    return pl.pallas_call(
        ready_kernel,
        out_shape=jax.ShapeDtypeStruct((ROWS, WIDTH), BF16),
        scratch_shapes=[pltpu.VMEM((1024, 128), F32)],
        compiler_params=pltpu.CompilerParams(vmem_limit_bytes=VMEM_LIMIT),
        cost_estimate=pl.CostEstimate(flops=2**28, bytes_accessed=2**19, transcendentals=0),
        name="ready",
    )(x, spread, diagonal)


def power_kernel(corpus_ref, out_ref):
    block = corpus_ref[...].astype(F32)
    total = block[:, :128] * block[:, :128]
    for r in range(1, 32):
        piece = block[:, r * 128 : (r + 1) * 128]
        total = total + piece * piece
    out_ref[...] = lax.dot_general(
        jnp.ones((8, 128), F32),
        total,
        (((1,), (1,)), ((), ())),
        precision=lax.Precision.HIGHEST,
        preferred_element_type=F32,
    )


def make_power(corpus):
    examples = corpus.shape[0]
    step = 256
    return pl.pallas_call(
        power_kernel,
        grid=(examples // step,),
        in_specs=[pl.BlockSpec((step, WIDTH), lambda i: (i, 0))],
        out_specs=pl.BlockSpec((8, step), lambda i: (0, i)),
        out_shape=jax.ShapeDtypeStruct((8, examples), F32),
        compiler_params=pltpu.CompilerParams(vmem_limit_bytes=VMEM_LIMIT),
        cost_estimate=pl.CostEstimate(flops=2**24, bytes_accessed=12 * 2**20, transcendentals=0),
        name="power",
    )(corpus)


def position(chunk):
    a, k, e = chunk
    dp, layer = lax.axis_index("dp"), lax.axis_index("layer")
    zl, x, c = (dp // 8 + a) % 2, (dp // 2 + 4 - k) % 4, (dp + e) % 2
    zh, y = zl * 2 + x // 2, (x % 2) * 2 + c
    return ((y + 4 - layer % 4) % 4) * 4 + zh


def dot_kernel(chunks, *refs):
    count = len(chunks)
    pieces, corpus_ref = refs[:count], refs[count]
    outs = refs[count + 1 : count + 5]
    rows, sems = refs[count + 5 :]

    @pl.when(pl.program_id(0) == 0)
    def _():
        copies = []
        for n, chunk in enumerate(chunks):
            start = pl.multiple_of(position(chunk) * ROWS, ROWS)
            copies.append(
                pltpu.make_async_copy(pieces[n], rows.at[pl.ds(start, ROWS)], sems.at[n])
            )
        for copy in copies:
            copy.start()
        for copy in copies:
            copy.wait()

    total = lax.dot_general(
        rows[...], corpus_ref[...], (((1,), (1,)), ((), ())), preferred_element_type=F32
    )
    for k in range(4):
        part = total[k * 128 : (k + 1) * 128].astype(BF16)
        outs[k][...] = part.reshape(4, ROWS, part.shape[1])


def make_totals(chunks, pieces, corpus):
    examples = corpus.shape[0]
    step = 256
    return pl.pallas_call(
        functools.partial(dot_kernel, chunks),
        grid=(examples // step,),
        in_specs=[any_space()] * len(chunks) + [pl.BlockSpec((step, WIDTH), lambda i: (i, 0))],
        out_specs=[pl.BlockSpec((4, ROWS, step), lambda i: (0, 0, i))] * 4,
        out_shape=[jax.ShapeDtypeStruct((4, ROWS, examples), BF16)] * 4,
        scratch_shapes=[
            pltpu.VMEM((512, WIDTH), BF16),
            pltpu.SemaphoreType.DMA((len(chunks),)),
        ],
        compiler_params=pltpu.CompilerParams(vmem_limit_bytes=VMEM_LIMIT),
        cost_estimate=pl.CostEstimate(
            flops=2 * 512 * examples * WIDTH, bytes_accessed=18 * 2**20, transcendentals=0
        ),
        name="totals",
    )(*pieces, corpus)


def add_kernel(*refs):
    ins, outs = refs[:4], refs[4:]
    zh = lax.axis_index("layer") // 4
    for m in range(4):
        at = (zh + m) % 4
        total = ins[0][at].astype(F32)
        for k in range(1, 4):
            total = total + ins[k][at].astype(F32)
        outs[m][...] = total.astype(outs[m].dtype)


def add_y(parts):
    examples = parts[0].shape[2]
    return pl.pallas_call(
        add_kernel,
        out_shape=[
            jax.ShapeDtypeStruct((ROWS, examples), F32 if m == 0 else BF16) for m in range(4)
        ],
        compiler_params=pltpu.CompilerParams(vmem_limit_bytes=VMEM_LIMIT),
        cost_estimate=pl.CostEstimate(flops=2**20, bytes_accessed=2 * 2**20, transcendentals=0),
        name="add_y",
    )(*parts)


def final_kernel(entries, own, a, b, c, p0, p1, p2, p3, out_ref):
    power = p0[0:1] + p1[0:1] + p2[0:1] + p3[0:1]
    factor = lax.rsqrt(power / entries + 1e-06)
    total = own[...] + a[...].astype(F32) + b[...].astype(F32) + c[...].astype(F32)
    out_ref[...] = (total * factor).reshape(out_ref.shape)


def finish(parts, powers, entries):
    examples = parts[0].shape[1]
    return pl.pallas_call(
        functools.partial(final_kernel, entries),
        out_shape=jax.ShapeDtypeStruct((16, 2, examples), F32),
        compiler_params=pltpu.CompilerParams(vmem_limit_bytes=VMEM_LIMIT),
        cost_estimate=pl.CostEstimate(flops=2**20, bytes_accessed=2**20, transcendentals=0),
        name="finish",
    )(*parts, *powers)


def per_device(query_grads, corpus_grads, left_inverse, right_inverse):
    corpus = corpus_grads.reshape(corpus_grads.shape[0], WIDTH)
    power = make_power(corpus)
    owned = lax.all_to_all(pack(query_grads[0]), "layer", 0, 0, tiled=True)
    own = make_ready(owned, left_inverse[0], right_inverse[0])

    pieces = {(0, 0): own}
    for k in (1, 3, 2):
        pieces[0, k] = shifted(own, x=k)
    pieces[1, 0] = shifted(own, zl=1)
    for k in (1, 3, 2):
        pieces[1, k] = shifted(pieces[1, 0], x=k)
    both = {}
    for (a, k), piece in pieces.items():
        both[a, k, 0] = piece
        both[a, k, 1] = shifted(piece, c=1)

    power = power + sum(shifted(power, y=k) for k in (1, 2, 3))
    powers = [power] + [shifted(power, zh=k) for k in (1, 2, 3)]

    chunks = list(both)
    totals = make_totals(chunks, [both[chunk] for chunk in chunks], corpus)
    parts = add_y([totals[0]] + [shifted(totals[k], y=k) for k in (1, 3, 2)])
    sums = [parts[0]] + [shifted(parts[m], zh=m) for m in (1, 3, 2)]
    return finish(sums, powers, WIDTH * LAYERS)


def solution(mesh):
    return jax.shard_map(
        per_device,
        mesh=mesh,
        in_specs=(
            P(("dp", "layer"), None, None, None),
            P("dp", "layer", None),
            P("layer", None, None),
            P("layer", None, None),
        ),
        out_specs=P("layer", None, "dp"),
        check_vma=False,
    )
```

time: 184 us -> 128 us (0.70)
  blocking collectives: 57.6 us -> 0 us
  starting transfers between devices: 0.04 us -> 44.4 us
  waiting for transfers between devices: 85.3 us -> 41.8 us
  Pallas kernels: 0 us -> 32.7 us
  matrix products: 14.5 us -> 0 us
  between operations: 13.5 us -> 0.28 us
  other arithmetic: 8.02 us -> 1.54 us
  local copies, waits for them, and re-layouts: 3.65 us -> 6.62 us
    reduce_scatter x1 -> x0, waiting for transfers between devices: 47.8 us -> none  [per_device(): lax.psum_scatter(total.reshape(share * lax.axis_size('layer'), groups, ex...]
    all_gather x1 -> x0, waiting for transfers between devices: 37.5 us -> none  [per_device(): lax.all_gather(precondition(owned, left_inverse, right_inverse), 'dp', ax...]
    psum x1 -> x0, blocking collectives: 35.8 us -> none  [per_device(): power = lax.psum(jnp.sum(wide * wide, axis=(1, 2)), 'layer')]
    ppermute x0 -> x27, waiting for transfers between devices: none -> 35.6 us  [shifted(): return lax.ppermute(value, ('dp', 'layer'), pairs)]
    ppermute x0 -> x27, starting transfers between devices: none -> 33.1 us  [shifted(): return lax.ppermute(value, ('dp', 'layer'), pairs)]
    pallas_call x0 -> x6, Pallas kernels: none -> 32.7 us  [the longest x1 13.2 us: make_totals(): pl.pallas_call(functools.partial(dot_kernel, chunks), grid=(examples // s...]
    all_to_all x1 -> x0, blocking collectives: 21.8 us -> none  [per_device(): lax.all_to_all(query_grads, 'layer', split_axis=2, concat_axis=0, tiled=T...]
    dot_general x3 -> x0, matrix products: 14.5 us -> none  [the longest x1 12.2 us: per_device(): lax.dot_general(flat, corpus_grads[:, 0, :], (((1,), (1,)), ((), ())), pr...]
  transfers between devices with their start and end apart: 2 -> 28, of which waited for: 2 -> 10; matrix products, arithmetic and copies ran while one was open for 4% -> 4% of each run, Pallas kernels for 0% -> 19%
where the time goes in v1:
time: 128 us; the launch traced here: 127 us
  starting transfers between devices  44.4 us (35%)
  waiting for transfers between devices  41.8 us (33%)
  Pallas kernels  32.7 us (26%)
  local copies, waits for them, and re-layouts  6.62 us (5%)
  other arithmetic  1.54 us (1%)
    ppermute x27, waiting for transfers between devices, shifted(): return lax.ppermute(value, ('dp', 'layer'), pairs)  35.6 us
    ppermute x27, starting transfers between devices, shifted(): return lax.ppermute(value, ('dp', 'layer'), pairs)  33.1 us
    pallas_call x1, Pallas kernels, make_totals(): pl.pallas_call(functools.partial(dot_kernel, chunks), grid=(examples // s...  13.2 us
    all_to_all x1, starting transfers between devices, per_device(): owned = lax.all_to_all(pack(query_grads[0]), 'layer', 0, 0, tiled=True)  11.3 us
    pallas_call x1, Pallas kernels, make_power(): pl.pallas_call(power_kernel, grid=(examples // step,), in_specs=[pl.Block...  8.46 us
    all_to_all x1, waiting for transfers between devices, per_device(): owned = lax.all_to_all(pack(query_grads[0]), 'layer', 0, 0, tiled=True)  6.17 us
    pallas_call x1, Pallas kernels, make_ready(): pl.pallas_call(ready_kernel, out_shape=jax.ShapeDtypeStruct((ROWS, WIDTH)...  4.86 us
    unnamed x54, local copies, waits for them, and re-layouts  3.69 us
  transfers between devices with their start and end apart: 28, of which 10 were waited for; matrix products, arithmetic and copies ran while one was open for 4% of the time, Pallas kernels for 19%

profile of v1, /device:TPU:24, one launch (start us, length us, event | category | flops | bytes accessed | tf_op | source)
XLA Modules:
  0.0 127.4 jit_solution(3930929353025649102)
XLA Ops:
  0.0 2.1 %pack.1 = bf16[16,64,128]{2,1,0:T(8,128)(2,1)} custom-call(bf16[2,16,4096]{2,1,0:T(8,128)(2,1)} %bitcast.8), custom_call_target="tpu_custom_call" | custom-call | bytes 524288 | tf_op jit(solution)/shard_map/pack/pallas_call | solution.py:44
  2.1 11.3 %all-to-all-start = ((bf16[16,64,128]{2,1,0:T(8,128)(2,1)}), bf16[16,64,128]{2,1,0:T(8,128)(2,1)S(1)}, u32[]{:S(2)}, u32[]{:S(2)}) async-start(bf16[16,64,128]{2,1,0:T(8,128)(2,1)} %pack.1), calls=%async_computation | async-start | bytes 524288 | tf_op jit(solution)/shard_map/all_to_all | solution.py:219
  13.4 1.8 %reshape_squeeze.3 = f32[32,2,32,2]{3,2,1,0:T(8,128)S(1)} reshape(f32[1,64,64]{2,1,0:T(8,128)} %param.6) | data formatting | bytes 32768 | tf_op jit(solution)/shard_map/reshape;squeeze | solution.py:77
  15.3 1.1 copy.6
  16.4 1.5 %select_maximum_fusion.right_ref = f32[128,128]{1,0:T(8,128)} fusion(f32[64,64]{1,0:T(8,128)} %bitcast.10), kind=kLoop, calls=%fused_computation | loop fusion | flops 81920 | bytes 81920 | tf_op jit(solution)/shard_map/concatenate | solution.py:74
  17.9 6.2 %all-to-all-done.x_ref = bf16[16,64,128]{2,1,0:T(8,128)(2,1)S(1)} async-done(((bf16[16,64,128]{2,1,0:T(8,128)(2,1)}), bf16[16,64,128]{2,1,0:T(8,128)(2,1)S(1)}, u32[]{:S(2)}, u32[]{:S(2)}) %all-to-all-start) | async-done | bytes 262176 | tf_op jit(solution)/shard_map/all_to_all | solution.py:219
  24.8 4.9 %ready.1.refs_0_ = bf16[32,4096]{1,0:T(8,128)(2,1)} custom-call(bf16[16,64,128]{2,1,0:T(8,128)(2,1)} %copy-done.3, f32[128,32]{1,0:T(8,128)} %bitcast.9, f32[128,128]{1,0:T(8,128)} %select_maximum_fusion.right_ref), custom_call_target="tpu_custom_call" | custom-call | flops 268435456 | bytes 524288 | tf_op jit(solution)/shard_map/ready/pallas_call | solution.py:78
  30.5 1.5 %collective-permute-start.1 = (bf16[32,4096]{1,0:T(8,128)(2,1)}, bf16[32,4096]{1,0:T(8,128)(2,1)S(1)}, u32[]{:S(2)}, u32[]{:S(2)}) collective-permute-start(bf16[32,4096]{1,0:T(8,128)(2,1)} %ready.1.refs_0_), channel_id=1, source_target_pairs={{0,32},{1,33},{2,34},{3,35},{4,36},{5,37},{6,38},{7,39},{8,40},{9,... | collective-permute-start | bytes 786440 | tf_op jit(solution)/shard_map/ppermute | solution.py:32
  31.9 1.7 %collective-permute-start.3 = (bf16[32,4096]{1,0:T(8,128)(2,1)}, bf16[32,4096]{1,0:T(8,128)(2,1)S(1)}, u32[]{:S(2)}, u32[]{:S(2)}) collective-permute-start(bf16[32,4096]{1,0:T(8,128)(2,1)} %ready.1.refs_0_), channel_id=1, source_target_pairs={{0,96},{1,97},{2,98},{3,99},{4,100},{5,101},{6,102},{7,103},{8,104... | collective-permute-start | bytes 786440 | tf_op jit(solution)/shard_map/ppermute | solution.py:32
  33.7 1.8 %collective-permute-start.5 = (bf16[32,4096]{1,0:T(8,128)(2,1)}, bf16[32,4096]{1,0:T(8,128)(2,1)S(1)}, u32[]{:S(2)}, u32[]{:S(2)}) collective-permute-start(bf16[32,4096]{1,0:T(8,128)(2,1)} %ready.1.refs_0_), channel_id=1, source_target_pairs={{0,64},{1,65},{2,66},{3,67},{4,68},{5,69},{6,70},{7,71},{8,72},{9,... | collective-permute-start | bytes 786440 | tf_op jit(solution)/shard_map/ppermute | solution.py:32
  36.2 1.5 %collective-permute-start.9 = (bf16[32,4096]{1,0:T(8,128)(2,1)S(1)}, bf16[32,4096]{1,0:T(8,128)(2,1)S(1)}, u32[]{:S(2)}, u32[]{:S(2)}) collective-permute-start(bf16[32,4096]{1,0:T(8,128)(2,1)S(1)} %collective-permute-done.7.refs_8_), channel_id=1, source_target_pairs={{0,32},{1,33},{2,34},{3,35},{4,36},{5,37},{6,38},{7,39},{8,40},{9,... | collective-permute-start | bytes 786440 | tf_op jit(solution)/shard_map/ppermute | solution.py:32
  37.7 4.0 %collective-permute-done.1.refs_2_ = bf16[32,4096]{1,0:T(8,128)(2,1)S(1)} collective-permute-done((bf16[32,4096]{1,0:T(8,128)(2,1)}, bf16[32,4096]{1,0:T(8,128)(2,1)S(1)}, u32[]{:S(2)}, u32[]{:S(2)}) %collective-permute-start.1) | collective-permute-done | bytes 262176 | tf_op jit(solution)/shard_map/ppermute | solution.py:32
  43.8 4.1 %collective-permute-done.5.refs_6_ = bf16[32,4096]{1,0:T(8,128)(2,1)S(1)} collective-permute-done((bf16[32,4096]{1,0:T(8,128)(2,1)}, bf16[32,4096]{1,0:T(8,128)(2,1)S(1)}, u32[]{:S(2)}, u32[]{:S(2)}) %collective-permute-start.5) | collective-permute-done | bytes 262176 | tf_op jit(solution)/shard_map/ppermute | solution.py:32
  48.3 3.7 %collective-permute-done.9.refs_10_ = bf16[32,4096]{1,0:T(8,128)(2,1)S(1)} collective-permute-done((bf16[32,4096]{1,0:T(8,128)(2,1)S(1)}, bf16[32,4096]{1,0:T(8,128)(2,1)S(1)}, u32[]{:S(2)}, u32[]{:S(2)}) %collective-permute-start.9) | collective-permute-done | bytes 262176 | tf_op jit(solution)/shard_map/ppermute | solution.py:32
  52.6 2.3 %collective-permute-done.13.refs_14_ = bf16[32,4096]{1,0:T(8,128)(2,1)S(1)} collective-permute-done((bf16[32,4096]{1,0:T(8,128)(2,1)S(1)}, bf16[32,4096]{1,0:T(8,128)(2,1)S(1)}, u32[]{:S(2)}, u32[]{:S(2)}) %collective-permute-start.13) | collective-permute-done | bytes 262176 | tf_op jit(solution)/shard_map/ppermute | solution.py:32
  55.7 8.5 %power.1 = f32[8,1536]{1,0:T(8,128)} custom-call(bf16[1536,4096]{1,0:T(8,128)(2,1)} %bitcast.5), custom_call_target="tpu_custom_call" | custom-call | flops 16777216 | bytes 12582912 | tf_op jit(solution)/shard_map/power/pallas_call | solution.py:106
  64.2 1.9 %collective-permute-start.21 = (f32[8,1536]{1,0:T(8,128)}, f32[8,1536]{1,0:T(8,128)S(1)}, u32[]{:S(2)}, u32[]{:S(2)}) collective-permute-start(f32[8,1536]{1,0:T(8,128)} %power.1), channel_id=1, source_target_pairs={{0,1},{1,2},{2,3},{3,0},{4,5},{5,6},{6,7},{7,4},{8,9},{9,10},{10,1... | collective-permute-start | bytes 147464 | tf_op jit(solution)/shard_map/ppermute | solution.py:32
  68.7 13.2 %totals.1 = (bf16[4,32,1536]{2,1,0:T(8,128)(2,1)}, bf16[4,32,1536]{2,1,0:T(8,128)(2,1)}, bf16[4,32,1536]{2,1,0:T(8,128)(2,1)}, bf16[4,32,1536]{2,1,0:T(8,128)(2,1)}) custom-call(bf16[32,4096]{1,0:T(8,128)(2,1)} %ready.1.refs_0_, bf16[32,4096]{1,0:T(8,128)(2,1)} %copy-done.16, bf16[32,4096]{1,0:T(8,128)(2,1)} %copy-done.13, bf16[32,4096]{1,0:T(8,128)(2,1)} %copy-done.21, ...), custom_call_target="tpu_custom_call" | custom-call | flops 6442450944 | bytes 18874368 | tf_op jit(solution)/shard_map/totals/pallas_call | solution.py:156
  82.0 3.2 %collective-permute-start.15 = (bf16[4,32,1536]{2,1,0:T(8,128)(2,1)}, bf16[4,32,1536]{2,1,0:T(8,128)(2,1)S(1)}, u32[]{:S(2)}, u32[]{:S(2)}) collective-permute-start(bf16[4,32,1536]{2,1,0:T(8,128)(2,1)} %get-tuple-element.14), channel_id=1, source_target_pairs={{0,1},{1,2},{2,3},{3,0},{4,5},{5,6},{6,7},{7,4},{8,9},{9,10},{10,1... | collective-permute-start | bytes 1179656 | tf_op jit(solution)/shard_map/ppermute | solution.py:32
  85.2 2.0 %collective-permute-start.17 = (bf16[4,32,1536]{2,1,0:T(8,128)(2,1)}, bf16[4,32,1536]{2,1,0:T(8,128)(2,1)S(1)}, u32[]{:S(2)}, u32[]{:S(2)}) collective-permute-start(bf16[4,32,1536]{2,1,0:T(8,128)(2,1)} %get-tuple-element.16), channel_id=1, source_target_pairs={{0,2},{1,3},{2,0},{3,1},{4,6},{5,7},{6,4},{7,5},{8,10},{9,11},{10,... | collective-permute-start | bytes 1179656 | tf_op jit(solution)/shard_map/ppermute | solution.py:32
  87.2 2.5 %collective-permute-start.24 = (f32[8,1536]{1,0:T(8,128)S(1)}, f32[8,1536]{1,0:T(8,128)S(1)}, u32[]{:S(2)}, u32[]{:S(2)}) collective-permute-start(f32[8,1536]{1,0:T(8,128)S(1)} %add_add_fusion.p0), channel_id=1, source_target_pairs={{0,4},{1,5},{2,6},{3,7},{4,8},{5,9},{6,10},{7,11},{8,12},{9,13},{1... | collective-permute-start | bytes 147464 | tf_op jit(solution)/shard_map/ppermute | solution.py:32
  89.7 12.2 %collective-permute-done.15.refs_1_ = bf16[4,32,1536]{2,1,0:T(8,128)(2,1)S(1)} collective-permute-done((bf16[4,32,1536]{2,1,0:T(8,128)(2,1)}, bf16[4,32,1536]{2,1,0:T(8,128)(2,1)S(1)}, u32[]{:S(2)}, u32[]{:S(2)}) %collective-permute-start.15) | collective-permute-done | bytes 393248 | tf_op jit(solution)/shard_map/ppermute | solution.py:32
  101.9 3.3 %collective-permute-done.16.refs_2_ = bf16[4,32,1536]{2,1,0:T(8,128)(2,1)S(1)} collective-permute-done((bf16[4,32,1536]{2,1,0:T(8,128)(2,1)}, bf16[4,32,1536]{2,1,0:T(8,128)(2,1)S(1)}, u32[]{:S(2)}, u32[]{:S(2)}) %collective-permute-start.16) | collective-permute-done | bytes 393248 | tf_op jit(solution)/shard_map/ppermute | solution.py:32
  106.1 2.2 %add_y.1 = (f32[32,1536]{1,0:T(8,128)}, bf16[32,1536]{1,0:T(8,128)(2,1)}, bf16[32,1536]{1,0:T(8,128)(2,1)}, bf16[32,1536]{1,0:T(8,128)(2,1)}) custom-call(bf16[4,32,1536]{2,1,0:T(8,128)(2,1)} %get-tuple-element.13.refs_0_, bf16[4,32,1536]{2,1,0:T(8,128)(2,1)} %copy-done, bf16[4,32,1536]{2,1,0:T(8,128)(2,1)} %copy-done.1, bf16[4,32,1536]{2,1,0:T(8,128)(2,1)} %copy-done.2), custom_call_target="tpu_custom_call" | custom-call | flops 1048576 | bytes 2097152 | tf_op jit(solution)/shard_map/add_y/pallas_call | solution.py:187
  108.3 2.7 %collective-permute-start.18 = (bf16[32,1536]{1,0:T(8,128)(2,1)}, bf16[32,1536]{1,0:T(8,128)(2,1)S(1)}, u32[]{:S(2)}, u32[]{:S(2)}) collective-permute-start(bf16[32,1536]{1,0:T(8,128)(2,1)} %get-tuple-element.18), channel_id=1, source_target_pairs={{0,4},{1,5},{2,6},{3,7},{4,8},{5,9},{6,10},{7,11},{8,12},{9,13},{1... | collective-permute-start | bytes 294920 | tf_op jit(solution)/shard_map/ppermute | solution.py:32
  111.0 1.4 %collective-permute-start.19 = (bf16[32,1536]{1,0:T(8,128)(2,1)}, bf16[32,1536]{1,0:T(8,128)(2,1)S(1)}, u32[]{:S(2)}, u32[]{:S(2)}) collective-permute-start(bf16[32,1536]{1,0:T(8,128)(2,1)} %get-tuple-element.19), channel_id=1, source_target_pairs={{0,12},{1,13},{2,14},{3,15},{4,0},{5,1},{6,2},{7,3},{8,4},{9,5},{1... | collective-permute-start | bytes 294920 | tf_op jit(solution)/shard_map/ppermute | solution.py:32
  112.5 3.0 %collective-permute-start.20 = (bf16[32,1536]{1,0:T(8,128)(2,1)}, bf16[32,1536]{1,0:T(8,128)(2,1)S(1)}, u32[]{:S(2)}, u32[]{:S(2)}) collective-permute-start(bf16[32,1536]{1,0:T(8,128)(2,1)} %get-tuple-element.20), channel_id=1, source_target_pairs={{0,8},{1,9},{2,10},{3,11},{4,12},{5,13},{6,14},{7,15},{8,0},{9,1},... | collective-permute-start | bytes 294920 | tf_op jit(solution)/shard_map/ppermute | solution.py:32
  115.5 2.9 %collective-permute-start.25 = (f32[8,1536]{1,0:T(8,128)S(1)}, f32[8,1536]{1,0:T(8,128)S(1)}, u32[]{:S(2)}, u32[]{:S(2)}) collective-permute-start(f32[8,1536]{1,0:T(8,128)S(1)} %add_add_fusion.p0), channel_id=1, source_target_pairs={{0,8},{1,9},{2,10},{3,11},{4,12},{5,13},{6,14},{7,15},{8,0},{9,1},... | collective-permute-start | bytes 147464 | tf_op jit(solution)/shard_map/ppermute | solution.py:32
  118.4 1.1 collective-permute-start.26
  119.5 4.0 %collective-permute-done.25.p2 = f32[8,1536]{1,0:T(8,128)S(1)} collective-permute-done((f32[8,1536]{1,0:T(8,128)S(1)}, f32[8,1536]{1,0:T(8,128)S(1)}, u32[]{:S(2)}, u32[]{:S(2)}) %collective-permute-start.25) | collective-permute-done | bytes 49184 | tf_op jit(solution)/shard_map/ppermute | solution.py:32
  123.5 1.3 %collective-permute-done.26.p3 = f32[8,1536]{1,0:T(8,128)S(1)} collective-permute-done((f32[8,1536]{1,0:T(8,128)S(1)}, f32[8,1536]{1,0:T(8,128)S(1)}, u32[]{:S(2)}, u32[]{:S(2)}) %collective-permute-start.26) | collective-permute-done | bytes 49184 | tf_op jit(solution)/shard_map/ppermute | solution.py:32
  125.6 1.9 %finish.1 = f32[16,2,1536]{2,1,0:T(2,128)} custom-call(f32[32,1536]{1,0:T(8,128)} %get-tuple-element.17.own, bf16[32,1536]{1,0:T(8,128)(2,1)} %copy-done.6, bf16[32,1536]{1,0:T(8,128)(2,1)} %copy-done.7, bf16[32,1536]{1,0:T(8,128)(2,1)} %copy-done.8, f32[8,1536]{1,0:T(8,128)} %copy-done.5, f32[8,1536]{1,0:T(8,128)} %copy-done.9, f32[8,1536]{1,0:T(8,128)} %copy-done.10, ...), custom_call_target="tpu_custom_call" | custom-call | flops 1048576 | bytes 1048576 | tf_op jit(solution)/shard_map/finish/pallas_call | solution.py:207
  (88 shorter events, 10.2 us)
Async XLA Ops:
  2.1 22.0 %all-to-all-start = ((bf16[16,64,128]{2,1,0:T(8,128)(2,1)}), bf16[16,64,128]{2,1,0:T(8,128)(2,1)S(1)}, u32[]{:S(2)}, u32[]{:S(2)}) async-start(bf16[16,64,128]{2,1,0:T(8,128)(2,1)} %pack.1), calls=%async_computation | async-start | bytes 524288 | tf_op jit(solution)/shard_map/all_to_all | solution.py:219
  29.6 6.6 %collective-permute-start.7 = (bf16[32,4096]{1,0:T(8,128)(2,1)}, bf16[32,4096]{1,0:T(8,128)(2,1)S(1)}, u32[]{:S(2)}, u32[]{:S(2)}) collective-permute-start(bf16[32,4096]{1,0:T(8,128)(2,1)} %ready.1.refs_0_), channel_id=1, source_target_pairs={{0,128},{1,129},{2,130},{3,131},{4,132},{5,133},{6,134},{7,135},{8... | collective-permute-start | bytes 786440 | tf_op jit(solution)/shard_map/ppermute | solution.py:32
  30.5 11.3 %collective-permute-start.1 = (bf16[32,4096]{1,0:T(8,128)(2,1)}, bf16[32,4096]{1,0:T(8,128)(2,1)S(1)}, u32[]{:S(2)}, u32[]{:S(2)}) collective-permute-start(bf16[32,4096]{1,0:T(8,128)(2,1)} %ready.1.refs_0_), channel_id=1, source_target_pairs={{0,32},{1,33},{2,34},{3,35},{4,36},{5,37},{6,38},{7,39},{8,40},{9,... | collective-permute-start | bytes 786440 | tf_op jit(solution)/shard_map/ppermute | solution.py:32
  31.9 10.7 %collective-permute-start.3 = (bf16[32,4096]{1,0:T(8,128)(2,1)}, bf16[32,4096]{1,0:T(8,128)(2,1)S(1)}, u32[]{:S(2)}, u32[]{:S(2)}) collective-permute-start(bf16[32,4096]{1,0:T(8,128)(2,1)} %ready.1.refs_0_), channel_id=1, source_target_pairs={{0,96},{1,97},{2,98},{3,99},{4,100},{5,101},{6,102},{7,103},{8,104... | collective-permute-start | bytes 786440 | tf_op jit(solution)/shard_map/ppermute | solution.py:32
  33.7 14.1 %collective-permute-start.5 = (bf16[32,4096]{1,0:T(8,128)(2,1)}, bf16[32,4096]{1,0:T(8,128)(2,1)S(1)}, u32[]{:S(2)}, u32[]{:S(2)}) collective-permute-start(bf16[32,4096]{1,0:T(8,128)(2,1)} %ready.1.refs_0_), channel_id=1, source_target_pairs={{0,64},{1,65},{2,66},{3,67},{4,68},{5,69},{6,70},{7,71},{8,72},{9,... | collective-permute-start | bytes 786440 | tf_op jit(solution)/shard_map/ppermute | solution.py:32
  35.5 12.3 %collective-permute-start = (bf16[32,4096]{1,0:T(8,128)(2,1)}, bf16[32,4096]{1,0:T(8,128)(2,1)S(1)}, u32[]{:S(2)}, u32[]{:S(2)}) collective-permute-start(bf16[32,4096]{1,0:T(8,128)(2,1)} %ready.1.refs_0_), channel_id=1, source_target_pairs={{0,16},{1,17},{2,18},{3,19},{4,20},{5,21},{6,22},{7,23},{8,24},{9,... | collective-permute-start | bytes 786440 | tf_op jit(solution)/shard_map/ppermute | solution.py:32
  36.2 31.0 %copy-start.12 = (bf16[32,4096]{1,0:T(8,128)(2,1)}, bf16[32,4096]{1,0:T(8,128)(2,1)S(1)}, u32[]{:S(2)}) copy-start(bf16[32,4096]{1,0:T(8,128)(2,1)S(1)} %collective-permute-done.7.refs_8_) | copy-start | bytes 786436
  36.2 15.8 %collective-permute-start.9 = (bf16[32,4096]{1,0:T(8,128)(2,1)S(1)}, bf16[32,4096]{1,0:T(8,128)(2,1)S(1)}, u32[]{:S(2)}, u32[]{:S(2)}) collective-permute-start(bf16[32,4096]{1,0:T(8,128)(2,1)S(1)} %collective-permute-done.7.refs_8_), channel_id=1, source_target_pairs={{0,32},{1,33},{2,34},{3,35},{4,36},{5,37},{6,38},{7,39},{8,40},{9,... | collective-permute-start | bytes 786440 | tf_op jit(solution)/shard_map/ppermute | solution.py:32
  41.7 25.5 %copy-start.13 = (bf16[32,4096]{1,0:T(8,128)(2,1)}, bf16[32,4096]{1,0:T(8,128)(2,1)S(1)}, u32[]{:S(2)}) copy-start(bf16[32,4096]{1,0:T(8,128)(2,1)S(1)} %collective-permute-done.1.refs_2_) | copy-start | bytes 786436
  41.7 10.3 %collective-permute-start.11 = (bf16[32,4096]{1,0:T(8,128)(2,1)S(1)}, bf16[32,4096]{1,0:T(8,128)(2,1)S(1)}, u32[]{:S(2)}, u32[]{:S(2)}) collective-permute-start(bf16[32,4096]{1,0:T(8,128)(2,1)S(1)} %collective-permute-done.7.refs_8_), channel_id=1, source_target_pairs={{0,96},{1,97},{2,98},{3,99},{4,100},{5,101},{6,102},{7,103},{8,104... | collective-permute-start | bytes 786440 | tf_op jit(solution)/shard_map/ppermute | solution.py:32
  42.7 24.6 %copy-start.14 = (bf16[32,4096]{1,0:T(8,128)(2,1)}, bf16[32,4096]{1,0:T(8,128)(2,1)S(1)}, u32[]{:S(2)}) copy-start(bf16[32,4096]{1,0:T(8,128)(2,1)S(1)} %collective-permute-done.3.refs_4_) | copy-start | bytes 786436
  42.7 12.2 %collective-permute-start.13 = (bf16[32,4096]{1,0:T(8,128)(2,1)S(1)}, bf16[32,4096]{1,0:T(8,128)(2,1)S(1)}, u32[]{:S(2)}, u32[]{:S(2)}) collective-permute-start(bf16[32,4096]{1,0:T(8,128)(2,1)S(1)} %collective-permute-done.7.refs_8_), channel_id=1, source_target_pairs={{0,64},{1,65},{2,66},{3,67},{4,68},{5,69},{6,70},{7,71},{8,72},{9,... | collective-permute-start | bytes 786440 | tf_op jit(solution)/shard_map/ppermute | solution.py:32
  47.8 7.1 %collective-permute-start.8 = (bf16[32,4096]{1,0:T(8,128)(2,1)S(1)}, bf16[32,4096]{1,0:T(8,128)(2,1)S(1)}, u32[]{:S(2)}, u32[]{:S(2)}) collective-permute-start(bf16[32,4096]{1,0:T(8,128)(2,1)S(1)} %collective-permute-done.7.refs_8_), channel_id=1, source_target_pairs={{0,16},{1,17},{2,18},{3,19},{4,20},{5,21},{6,22},{7,23},{8,24},{9,... | collective-permute-start | bytes 786440 | tf_op jit(solution)/shard_map/ppermute | solution.py:32
  47.8 7.6 %collective-permute-start.2 = (bf16[32,4096]{1,0:T(8,128)(2,1)S(1)}, bf16[32,4096]{1,0:T(8,128)(2,1)S(1)}, u32[]{:S(2)}, u32[]{:S(2)}) collective-permute-start(bf16[32,4096]{1,0:T(8,128)(2,1)S(1)} %collective-permute-done.1.refs_2_), channel_id=1, source_target_pairs={{0,16},{1,17},{2,18},{3,19},{4,20},{5,21},{6,22},{7,23},{8,24},{9,... | collective-permute-start | bytes 786440 | tf_op jit(solution)/shard_map/ppermute | solution.py:32
  52.0 12.1 %collective-permute-start.4 = (bf16[32,4096]{1,0:T(8,128)(2,1)S(1)}, bf16[32,4096]{1,0:T(8,128)(2,1)S(1)}, u32[]{:S(2)}, u32[]{:S(2)}) collective-permute-start(bf16[32,4096]{1,0:T(8,128)(2,1)S(1)} %collective-permute-done.3.refs_4_), channel_id=1, source_target_pairs={{0,16},{1,17},{2,18},{3,19},{4,20},{5,21},{6,22},{7,23},{8,24},{9,... | collective-permute-start | bytes 786440 | tf_op jit(solution)/shard_map/ppermute | solution.py:32
  52.1 14.0 %collective-permute-start.6 = (bf16[32,4096]{1,0:T(8,128)(2,1)S(1)}, bf16[32,4096]{1,0:T(8,128)(2,1)S(1)}, u32[]{:S(2)}, u32[]{:S(2)}) collective-permute-start(bf16[32,4096]{1,0:T(8,128)(2,1)S(1)} %collective-permute-done.5.refs_6_), channel_id=1, source_target_pairs={{0,16},{1,17},{2,18},{3,19},{4,20},{5,21},{6,22},{7,23},{8,24},{9,... | collective-permute-start | bytes 786440 | tf_op jit(solution)/shard_map/ppermute | solution.py:32
  54.9 12.3 %collective-permute-start.10 = (bf16[32,4096]{1,0:T(8,128)(2,1)S(1)}, bf16[32,4096]{1,0:T(8,128)(2,1)S(1)}, u32[]{:S(2)}, u32[]{:S(2)}) collective-permute-start(bf16[32,4096]{1,0:T(8,128)(2,1)S(1)} %collective-permute-done.9.refs_10_), channel_id=1, source_target_pairs={{0,16},{1,17},{2,18},{3,19},{4,20},{5,21},{6,22},{7,23},{8,24},{9,... | collective-permute-start | bytes 786440 | tf_op jit(solution)/shard_map/ppermute | solution.py:32
  54.9 12.3 %collective-permute-start.12 = (bf16[32,4096]{1,0:T(8,128)(2,1)S(1)}, bf16[32,4096]{1,0:T(8,128)(2,1)S(1)}, u32[]{:S(2)}, u32[]{:S(2)}) collective-permute-start(bf16[32,4096]{1,0:T(8,128)(2,1)S(1)} %collective-permute-done.11.refs_12_), channel_id=1, source_target_pairs={{0,16},{1,17},{2,18},{3,19},{4,20},{5,21},{6,22},{7,23},{8,24},{9,... | collective-permute-start | bytes 786440 | tf_op jit(solution)/shard_map/ppermute | solution.py:32
  55.4 11.8 %collective-permute-start.14 = (bf16[32,4096]{1,0:T(8,128)(2,1)S(1)}, bf16[32,4096]{1,0:T(8,128)(2,1)S(1)}, u32[]{:S(2)}, u32[]{:S(2)}) collective-permute-start(bf16[32,4096]{1,0:T(8,128)(2,1)S(1)} %collective-permute-done.13.refs_14_), channel_id=1, source_target_pairs={{0,16},{1,17},{2,18},{3,19},{4,20},{5,21},{6,22},{7,23},{8,24},{9,... | collective-permute-start | bytes 786440 | tf_op jit(solution)/shard_map/ppermute | solution.py:32
  64.2 21.0 %collective-permute-start.21 = (f32[8,1536]{1,0:T(8,128)}, f32[8,1536]{1,0:T(8,128)S(1)}, u32[]{:S(2)}, u32[]{:S(2)}) collective-permute-start(f32[8,1536]{1,0:T(8,128)} %power.1), channel_id=1, source_target_pairs={{0,1},{1,2},{2,3},{3,0},{4,5},{5,6},{6,7},{7,4},{8,9},{9,10},{10,1... | collective-permute-start | bytes 147464 | tf_op jit(solution)/shard_map/ppermute | solution.py:32
  66.1 21.1 %collective-permute-start.22 = (f32[8,1536]{1,0:T(8,128)}, f32[8,1536]{1,0:T(8,128)S(1)}, u32[]{:S(2)}, u32[]{:S(2)}) collective-permute-start(f32[8,1536]{1,0:T(8,128)} %power.1), channel_id=1, source_target_pairs={{0,2},{1,3},{2,0},{3,1},{4,6},{5,7},{6,4},{7,5},{8,10},{9,11},{10,... | collective-permute-start | bytes 147464 | tf_op jit(solution)/shard_map/ppermute | solution.py:32
  67.2 20.0 %collective-permute-start.23 = (f32[8,1536]{1,0:T(8,128)}, f32[8,1536]{1,0:T(8,128)S(1)}, u32[]{:S(2)}, u32[]{:S(2)}) collective-permute-start(f32[8,1536]{1,0:T(8,128)} %power.1), channel_id=1, source_target_pairs={{0,3},{1,0},{2,1},{3,2},{4,7},{5,4},{6,5},{7,6},{8,11},{9,8},{10,9... | collective-permute-start | bytes 147464 | tf_op jit(solution)/shard_map/ppermute | solution.py:32
  82.0 19.9 %collective-permute-start.15 = (bf16[4,32,1536]{2,1,0:T(8,128)(2,1)}, bf16[4,32,1536]{2,1,0:T(8,128)(2,1)S(1)}, u32[]{:S(2)}, u32[]{:S(2)}) collective-permute-start(bf16[4,32,1536]{2,1,0:T(8,128)(2,1)} %get-tuple-element.14), channel_id=1, source_target_pairs={{0,1},{1,2},{2,3},{3,0},{4,5},{5,6},{6,7},{7,4},{8,9},{9,10},{10,1... | collective-permute-start | bytes 1179656 | tf_op jit(solution)/shard_map/ppermute | solution.py:32
  85.2 20.0 %collective-permute-start.16 = (bf16[4,32,1536]{2,1,0:T(8,128)(2,1)}, bf16[4,32,1536]{2,1,0:T(8,128)(2,1)S(1)}, u32[]{:S(2)}, u32[]{:S(2)}) collective-permute-start(bf16[4,32,1536]{2,1,0:T(8,128)(2,1)} %get-tuple-element.15), channel_id=1, source_target_pairs={{0,3},{1,0},{2,1},{3,2},{4,7},{5,4},{6,5},{7,6},{8,11},{9,8},{10,9... | collective-permute-start | bytes 1179656 | tf_op jit(solution)/shard_map/ppermute | solution.py:32
  85.2 20.0 %collective-permute-start.17 = (bf16[4,32,1536]{2,1,0:T(8,128)(2,1)}, bf16[4,32,1536]{2,1,0:T(8,128)(2,1)S(1)}, u32[]{:S(2)}, u32[]{:S(2)}) collective-permute-start(bf16[4,32,1536]{2,1,0:T(8,128)(2,1)} %get-tuple-element.16), channel_id=1, source_target_pairs={{0,2},{1,3},{2,0},{3,1},{4,6},{5,7},{6,4},{7,5},{8,10},{9,11},{10,... | collective-permute-start | bytes 1179656 | tf_op jit(solution)/shard_map/ppermute | solution.py:32
  87.2 37.7 %copy-start.5 = (f32[8,1536]{1,0:T(8,128)}, f32[8,1536]{1,0:T(8,128)S(1)}, u32[]{:S(2)}) copy-start(f32[8,1536]{1,0:T(8,128)S(1)} %add_add_fusion.p0) | copy-start | bytes 147460
  87.2 31.2 %collective-permute-start.24 = (f32[8,1536]{1,0:T(8,128)S(1)}, f32[8,1536]{1,0:T(8,128)S(1)}, u32[]{:S(2)}, u32[]{:S(2)}) collective-permute-start(f32[8,1536]{1,0:T(8,128)S(1)} %add_add_fusion.p0), channel_id=1, source_target_pairs={{0,4},{1,5},{2,6},{3,7},{4,8},{5,9},{6,10},{7,11},{8,12},{9,13},{1... | collective-permute-start | bytes 147464 | tf_op jit(solution)/shard_map/ppermute | solution.py:32
  108.3 16.5 %collective-permute-start.18 = (bf16[32,1536]{1,0:T(8,128)(2,1)}, bf16[32,1536]{1,0:T(8,128)(2,1)S(1)}, u32[]{:S(2)}, u32[]{:S(2)}) collective-permute-start(bf16[32,1536]{1,0:T(8,128)(2,1)} %get-tuple-element.18), channel_id=1, source_target_pairs={{0,4},{1,5},{2,6},{3,7},{4,8},{5,9},{6,10},{7,11},{8,12},{9,13},{1... | collective-permute-start | bytes 294920 | tf_op jit(solution)/shard_map/ppermute | solution.py:32
  111.0 13.8 %collective-permute-start.19 = (bf16[32,1536]{1,0:T(8,128)(2,1)}, bf16[32,1536]{1,0:T(8,128)(2,1)S(1)}, u32[]{:S(2)}, u32[]{:S(2)}) collective-permute-start(bf16[32,1536]{1,0:T(8,128)(2,1)} %get-tuple-element.19), channel_id=1, source_target_pairs={{0,12},{1,13},{2,14},{3,15},{4,0},{5,1},{6,2},{7,3},{8,4},{9,5},{1... | collective-permute-start | bytes 294920 | tf_op jit(solution)/shard_map/ppermute | solution.py:32
  112.5 12.4 %collective-permute-start.20 = (bf16[32,1536]{1,0:T(8,128)(2,1)}, bf16[32,1536]{1,0:T(8,128)(2,1)S(1)}, u32[]{:S(2)}, u32[]{:S(2)}) collective-permute-start(bf16[32,1536]{1,0:T(8,128)(2,1)} %get-tuple-element.20), channel_id=1, source_target_pairs={{0,8},{1,9},{2,10},{3,11},{4,12},{5,13},{6,14},{7,15},{8,0},{9,1},... | collective-permute-start | bytes 294920 | tf_op jit(solution)/shard_map/ppermute | solution.py:32
  115.5 8.0 %collective-permute-start.25 = (f32[8,1536]{1,0:T(8,128)S(1)}, f32[8,1536]{1,0:T(8,128)S(1)}, u32[]{:S(2)}, u32[]{:S(2)}) collective-permute-start(f32[8,1536]{1,0:T(8,128)S(1)} %add_add_fusion.p0), channel_id=1, source_target_pairs={{0,8},{1,9},{2,10},{3,11},{4,12},{5,13},{6,14},{7,15},{8,0},{9,1},... | collective-permute-start | bytes 147464 | tf_op jit(solution)/shard_map/ppermute | solution.py:32
  118.4 6.4 %collective-permute-start.26 = (f32[8,1536]{1,0:T(8,128)S(1)}, f32[8,1536]{1,0:T(8,128)S(1)}, u32[]{:S(2)}, u32[]{:S(2)}) collective-permute-start(f32[8,1536]{1,0:T(8,128)S(1)} %add_add_fusion.p0), channel_id=1, source_target_pairs={{0,12},{1,13},{2,14},{3,15},{4,0},{5,1},{6,2},{7,3},{8,4},{9,5},{1... | collective-permute-start | bytes 147464 | tf_op jit(solution)/shard_map/ppermute | solution.py:32
  (23 other events, 152.0 us)

commit v2 on v0

v2 whole, which is shorter than its diff:
```python
import functools

import jax
import jax.numpy as jnp
from jax import lax
from jax.experimental import pallas as pl
from jax.experimental.pallas import tpu as pltpu
from jax.sharding import PartitionSpec as P

F32, BF16 = jnp.float32, jnp.bfloat16
SIZES = {"zl": 2, "x": 4, "c": 2, "zh": 4, "y": 4}
ROWS, WIDTH, LAYERS = 32, 4096, 16
MIB = 1024 * 1024
FETCHES, AHEAD, PARTS = 3, 2, 16
VMEM = pl.BlockSpec(memory_space=pltpu.VMEM)


def kernel_call(body, name, out_shape, args, flops, moved, limit=4, **more):
    single = not isinstance(out_shape, list)
    return pl.pallas_call(
        body,
        in_specs=[VMEM] * len(args),
        out_specs=VMEM if single else [VMEM] * len(out_shape),
        out_shape=out_shape,
        compiler_params=pltpu.CompilerParams(vmem_limit_bytes=limit * MIB),
        cost_estimate=pl.CostEstimate(flops=flops, bytes_accessed=moved, transcendentals=0),
        name=name,
        **more,
    )(*args)


def shape(*sizes, dtype=BF16):
    return jax.ShapeDtypeStruct(sizes, dtype)


def shifted(value, keep=None, **shift):
    pairs = []
    for index in range(256):
        dp, layer = divmod(index, 16)
        at = {"zl": dp // 8, "x": dp // 2 % 4, "c": dp % 2, "zh": layer // 4, "y": layer % 4}
        for name, by in shift.items():
            at[name] = (at[name] + by) % SIZES[name]
        if keep is None or keep(at):
            to = (at["zl"] * 8 + at["x"] * 2 + at["c"]) * 16 + at["zh"] * 4 + at["y"]
            pairs.append((index, to))
    return lax.ppermute(value, ("dp", "layer"), pairs)


def pack_kernel(x_ref, out_ref, scratch):
    for b in range(2):
        for r in range(32):
            piece = x_ref[b, :, r * 128 : (r + 1) * 128].astype(F32)
            scratch[pl.ds(b * 32 + r, LAYERS, stride=64), :] = piece
    out_ref[...] = scratch[...].astype(BF16).reshape(LAYERS, 64, 128)


def pack(x):
    return kernel_call(
        pack_kernel,
        "pack",
        shape(LAYERS, 64, 128),
        [x],
        0,
        2**19,
        scratch_shapes=[pltpu.VMEM((LAYERS * 64, 128), F32)],
    )


def split(value, count):
    pieces = []
    for _ in range(count):
        piece = value.astype(BF16)
        value = value - piece.astype(F32)
        pieces.append(piece)
    return pieces


def product(a, b):
    return jnp.dot(a, b, preferred_element_type=F32)


def factors_kernel(left_ref, right_ref, left_out, right_out):
    row = lax.broadcasted_iota(jnp.int32, (64, 128), 0)
    lane = lax.broadcasted_iota(jnp.int32, (64, 128), 1) % 64
    twice = jnp.where(row == lane, 1.0, 0.0).astype(BF16)
    spread = jnp.where(row == 2 * (lane % 32) + lane // 32, 1.0, 0.0).astype(BF16)
    row = lax.broadcasted_iota(jnp.int32, (64, 64), 0)
    lane = lax.broadcasted_iota(jnp.int32, (64, 64), 1)
    gather = jnp.where(lane == 2 * (row % 32) + row // 32, 1.0, 0.0).astype(BF16)
    zero = jnp.zeros((64, 128), BF16)
    for n, piece in enumerate(split(right_ref[...], 3)):
        double = product(piece, twice).astype(BF16)
        right_out[0:64, n * 256 : n * 256 + 128] = double
        right_out[0:64, n * 256 + 128 : n * 256 + 256] = zero
        right_out[64:128, n * 256 : n * 256 + 128] = zero
        right_out[64:128, n * 256 + 128 : n * 256 + 256] = double
    for n, piece in enumerate(split(left_ref[...], 2)):
        rows = product(gather, piece).astype(BF16)
        left_out[:, n * 128 : (n + 1) * 128] = product(rows, spread).astype(BF16)


def make_factors(left, right):
    return kernel_call(
        factors_kernel,
        "factors",
        [shape(64, 256), shape(128, 768)],
        [left, right],
        2**22,
        2**18,
    )


def ready_kernel(x_ref, left_ref, right_ref, out_ref, scratch):
    x = x_ref[...].reshape(16 * 64, 128)
    y = product(x, right_ref[:, 0:256])
    y = y + product(x, right_ref[:, 256:512])
    y = y + product(x, right_ref[:, 512:768])
    high = y.astype(BF16)
    low = (y - high.astype(F32)).astype(BF16)
    stacks = []
    for i in range(32):
        at = slice(i * 32, (i + 1) * 32)
        column = jnp.concatenate(
            [high[at, :128], high[at, 128:], low[at, :128], low[at, 128:]], axis=0
        )
        stacks.append(jnp.concatenate([column, column], axis=0))
    z = product(left_ref[...], jnp.concatenate(stacks, axis=1))
    first = lax.broadcasted_iota(jnp.int32, (32, 128), 1) < 64
    for i in range(32):
        part = z[:, i * 128 : (i + 1) * 128]
        scratch[i * 32 : (i + 1) * 32, :] = jnp.where(first, part[0:32], part[32:64])
    for r in range(32):
        out_ref[:, r * 128 : (r + 1) * 128] = scratch[pl.ds(r, 32, stride=32), :].astype(BF16)


def make_ready(x, left, right):
    return kernel_call(
        ready_kernel,
        "ready",
        shape(ROWS, WIDTH),
        [x, left, right],
        2**28,
        2**19,
        scratch_shapes=[pltpu.VMEM((1024, 128), F32)],
    )


def fetch(corpus_ref, held_ref, sems, use):
    count = sems.shape[0]
    step = corpus_ref.shape[0] // count

    def copy(start, size, n):
        at = pl.ds(start, size)
        return pltpu.make_async_copy(corpus_ref.at[at], held_ref.at[at], sems.at[n])

    def begin(n):
        for part in range(PARTS):
            copy(n * step + part * step // PARTS, step // PARTS, n).start()

    for n in range(AHEAD):
        begin(n)
    for n in range(count):
        copy(n * step, step, n).wait()
        if n + AHEAD < count:
            begin(n + AHEAD)
        use(n * step, step)


def power_kernel(corpus_ref, out_ref, held_ref, sems):
    def use(start, step):
        totals = []
        for s in range(start, start + step, 32):
            total = None
            for r in range(32):
                piece = held_ref[s : s + 32, r * 128 : (r + 1) * 128].astype(F32)
                total = piece * piece if total is None else total + piece * piece
            totals.append(total)
        power = lax.dot_general(
            jnp.ones((8, 128), F32),
            jnp.concatenate(totals, axis=0),
            (((1,), (1,)), ((), ())),
            precision=lax.Precision.HIGHEST,
            preferred_element_type=F32,
        )[0:1]
        for j in range(step // 128):
            row = start // 128 + j
            out_ref[row : row + 1, :] = power[:, j * 128 : (j + 1) * 128]

    fetch(corpus_ref, held_ref, sems, use)


def corpus_call(body, name, out_shape, args, flops, scratch, limit=50):
    single = not isinstance(out_shape, list)
    return pl.pallas_call(
        body,
        in_specs=[VMEM] * (len(args) - 1) + [pl.BlockSpec(memory_space=pl.ANY)],
        out_specs=VMEM if single else [VMEM] * len(out_shape),
        out_shape=out_shape,
        scratch_shapes=[*scratch, pltpu.SemaphoreType.DMA((FETCHES,))],
        compiler_params=pltpu.CompilerParams(vmem_limit_bytes=limit * MIB),
        cost_estimate=pl.CostEstimate(
            flops=flops, bytes_accessed=13 * MIB, transcendentals=0
        ),
        name=name,
    )(*args)


def make_power(corpus):
    out = shape(corpus.shape[0] // 128, 128, dtype=F32)
    held = pltpu.VMEM(corpus.shape, BF16)
    return corpus_call(power_kernel, "power", out, [corpus], 2**27, [held])


HALVES = (((0, 0), (0, 1), (0, 3), (1, 0)), ((0, 2), (1, 1), (1, 3), (1, 2)))


def position(chunk):
    a, k, e = chunk
    dp, layer = lax.axis_index("dp"), lax.axis_index("layer")
    x, c = (dp // 2 + 4 - k) % 4, (dp + e) % 2
    block = a if k % 2 == 0 else x // 2
    return (((x % 2) * 2 + c + 4 - layer % 4) % 4) * 2 + block


def place(zh):
    dp, layer = lax.axis_index("dp"), lax.axis_index("layer")
    zl, x, y = dp // 8, dp // 2 % 4, layer % 4
    other = (zh // 2 + zl) % 2
    even = (y // 2 + x) % 2 == 0
    half = jnp.where(even, (zh + x // 2) % 2, other)
    return half, jnp.where(even, other, zh % 2)


def power_rows(power):
    high = power.astype(BF16).astype(F32)
    rest = jnp.zeros((ROWS - 2 * power.shape[0], 128), F32)
    return jnp.concatenate([high, power - high, rest], axis=0).astype(BF16)


def power_of(block, count):
    block = block.astype(F32)
    return block[:count] + block[count : 2 * count]


def dot_block(chunks, pieces, corpus_ref, held, start, step):
    at = pl.ds(start, step)
    rows = jnp.concatenate([piece[...] for piece in pieces], axis=0)
    total = lax.dot_general(
        rows, corpus_ref[at], (((1,), (1,)), ((), ())), preferred_element_type=F32
    ).astype(BF16)
    for j, chunk in enumerate(chunks):
        held[position(chunk), :, at] = total[j * ROWS : (j + 1) * ROWS]


def first_kernel(chunks, *refs):
    count = len(chunks)
    pieces, power_ref, corpus_ref = refs[:count], refs[count], refs[count + 1]
    outs, (corpus, held, sems) = refs[count + 2 : -3], refs[-3:]
    fetch(corpus_ref, corpus, sems, functools.partial(dot_block, chunks, pieces, corpus, held))
    examples = corpus_ref.shape[0]
    power = power_rows(power_ref[...])
    for k in range(4):
        outs[k][:, :, :examples] = held[2 * k : 2 * k + 2]
        outs[k][0, :, examples:] = power
        outs[k][1, :, examples:] = power


def make_first(chunks, pieces, power, corpus):
    examples = corpus.shape[0]
    *totals, held = corpus_call(
        functools.partial(first_kernel, chunks),
        "first",
        [shape(2, ROWS, examples + 128)] * 4 + [shape(examples, WIDTH)],
        [*pieces, power, corpus],
        2 * 256 * examples * WIDTH,
        [pltpu.VMEM((8, ROWS, examples), BF16)],
        30,
    )
    return totals, held


def second_kernel(chunks, *refs):
    count = len(chunks)
    pieces, corpus_ref, outs, held = refs[:count], refs[count], refs[count + 1 : -1], refs[-1]
    for start in range(0, corpus_ref.shape[0], 256):
        dot_block(chunks, pieces, corpus_ref, held, start, 256)
    for k in range(4):
        outs[k][...] = held[2 * k : 2 * k + 2]


def make_second(chunks, pieces, corpus):
    examples = corpus.shape[0]
    return kernel_call(
        functools.partial(second_kernel, chunks),
        "second",
        [shape(2, ROWS, examples)] * 4,
        [*pieces, corpus],
        2 * 256 * examples * WIDTH,
        15 * MIB,
        scratch_shapes=[pltpu.VMEM((8, ROWS, examples), BF16)],
    )


def add_kernel(*refs):
    halves, outs = (refs[:4], refs[4:8]), refs[8:]
    zh = lax.axis_index("layer") // 4
    examples = halves[1][0].shape[2]
    count = examples // 128
    power = power_of(halves[0][0][0, :, examples:], count)
    for k in range(1, 4):
        power = power + power_of(halves[0][k][0, :, examples:], count)
    for m in range(4):
        half, block = place((zh + m) % 4)

        def add(parts):
            total = parts[0][block, :, :examples].astype(F32)
            for k in range(1, 4):
                total = total + parts[k][block, :, :examples].astype(F32)
            outs[m][:, :examples] = total.astype(outs[m].dtype)

        pl.when(half == 0)(functools.partial(add, halves[0]))
        pl.when(half == 1)(functools.partial(add, halves[1]))
        if m == 0:
            outs[m][0:count, examples:] = power
        else:
            outs[m][:, examples:] = power_rows(power)


def add_y(parts):
    examples = parts[4].shape[2]
    outs = [shape(ROWS, examples + 128, dtype=F32 if m == 0 else BF16) for m in range(4)]
    return kernel_call(add_kernel, "add_y", outs, parts, 2**20, 2 * MIB)


def final_kernel(entries, own, a, b, c, out_ref):
    examples = out_ref.shape[2]
    count = examples // 128
    power = own[0:count, examples:]
    for piece in (a, b, c):
        power = power + power_of(piece[:, examples:], count)
    factor = lax.rsqrt(power / entries + 1e-06)
    for j in range(count):
        at = slice(j * 128, (j + 1) * 128)
        total = own[:, at] + a[:, at].astype(F32) + b[:, at].astype(F32) + c[:, at].astype(F32)
        out_ref[:, :, at] = (total * factor[j : j + 1, :]).reshape(16, 2, 128)


def finish(parts, entries):
    examples = parts[0].shape[1] - 128
    return kernel_call(
        functools.partial(final_kernel, entries),
        "finish",
        shape(16, 2, examples, dtype=F32),
        parts,
        2**20,
        MIB,
    )


def per_device(query_grads, corpus_grads, left_inverse, right_inverse):
    corpus = corpus_grads.reshape(corpus_grads.shape[0], WIDTH)
    owned = lax.all_to_all(pack(query_grads[0]), "layer", 0, 0, tiled=True)
    power = make_power(corpus)
    left, right = make_factors(left_inverse[0], right_inverse[0])
    owned, power, left, right = lax.optimization_barrier((owned, power, left, right))
    own = make_ready(owned, left, right)

    other = shifted(own, zl=1)
    pieces = {(0, 0): own, (1, 0): other, (0, 1): shifted(own, x=1), (0, 3): shifted(own, x=3)}
    pieces[0, 2] = shifted(own, x=2)
    pieces[1, 1], pieces[1, 3] = shifted(other, x=1), shifted(other, x=3)
    pieces[1, 2] = shifted(pieces[0, 2], zl=1)

    mine = [pieces[chunk] for chunk in HALVES[0]]
    mine += [shifted(piece, c=1) for piece in mine]
    chunks = [(a, k, e) for e in (0, 1) for a, k in HALVES[0]]
    totals, held = make_first(chunks, mine, power, corpus)

    mine = [pieces[chunk] for chunk in HALVES[1]]
    mine, totals = lax.optimization_barrier((mine, totals))
    parts = [totals[0]] + [shifted(totals[k], y=k) for k in (1, 2, 3)]
    mine += [shifted(piece, c=1) for piece in mine]
    chunks = [(a, k, e) for e in (0, 1) for a, k in HALVES[1]]
    totals = make_second(chunks, mine, held)
    parts += [totals[0]] + [shifted(totals[k], y=k) for k in (1, 2, 3)]
    sums = add_y(parts)
    return finish([sums[0]] + [shifted(sums[m], zh=m) for m in (1, 2, 3)], WIDTH * LAYERS)


def solution(mesh):
    return jax.shard_map(
        per_device,
        mesh=mesh,
        in_specs=(
            P(("dp", "layer"), None, None, None),
            P("dp", "layer", None),
            P("layer", None, None),
            P("layer", None, None),
        ),
        out_specs=P("layer", None, "dp"),
        check_vma=False,
    )
```

time: 184 us -> 93.4 us (0.51)
  blocking collectives: 57.6 us -> 0 us
  waiting for transfers between devices: 85.3 us -> 35 us
  starting transfers between devices: 0.04 us -> 35.9 us
  Pallas kernels: 0 us -> 19.5 us
  matrix products: 14.5 us -> 0 us
  between operations: 13.5 us -> 0.1 us
  other arithmetic: 8.02 us -> 0 us
    reduce_scatter x1 -> x0, waiting for transfers between devices: 47.8 us -> none  [per_device(): lax.psum_scatter(total.reshape(share * lax.axis_size('layer'), groups, ex...]
    all_gather x1 -> x0, waiting for transfers between devices: 37.5 us -> none  [per_device(): lax.all_gather(precondition(owned, left_inverse, right_inverse), 'dp', ax...]
    psum x1 -> x0, blocking collectives: 35.8 us -> none  [per_device(): power = lax.psum(jnp.sum(wide * wide, axis=(1, 2)), 'layer')]
    ppermute x0 -> x24, waiting for transfers between devices: none -> 32.1 us  [shifted(): return lax.ppermute(value, ('dp', 'layer'), pairs)]
    ppermute x0 -> x24, starting transfers between devices: none -> 24.6 us  [shifted(): return lax.ppermute(value, ('dp', 'layer'), pairs)]
    all_to_all x1 -> x0, blocking collectives: 21.8 us -> none  [per_device(): lax.all_to_all(query_grads, 'layer', split_axis=2, concat_axis=0, tiled=T...]
    pallas_call x0 -> x8, Pallas kernels: none -> 19.5 us  [the longest x2 12 us: corpus_call(): pl.pallas_call(body, in_specs=[VMEM] * (len(args) - 1) + [pl.BlockSpec(me...]
    dot_general x3 -> x0, matrix products: 14.5 us -> none  [the longest x1 12.2 us: per_device(): lax.dot_general(flat, corpus_grads[:, 0, :], (((1,), (1,)), ((), ())), pr...]
  transfers between devices with their start and end apart: 2 -> 25, of which waited for: 2 -> 13; matrix products, arithmetic and copies ran while one was open for 4% -> 0% of each run, Pallas kernels for 0% -> 17%
where the time goes in v2:
time: 93.4 us; the launch traced here: 93 us
  starting transfers between devices  35.9 us (38%)
  waiting for transfers between devices  35 us (37%)
  Pallas kernels  19.5 us (21%)
  local copies, waits for them, and re-layouts  2.46 us (3%)
    ppermute x24, waiting for transfers between devices, shifted(): return lax.ppermute(value, ('dp', 'layer'), pairs)  32.1 us
    ppermute x24, starting transfers between devices, shifted(): return lax.ppermute(value, ('dp', 'layer'), pairs)  24.6 us
    pallas_call x2, Pallas kernels, corpus_call(): pl.pallas_call(body, in_specs=[VMEM] * (len(args) - 1) + [pl.BlockSpec(me...  12 us
    all_to_all x1, starting transfers between devices, per_device(): owned = lax.all_to_all(pack(query_grads[0]), 'layer', 0, 0, tiled=True)  11.3 us
    pallas_call x6, Pallas kernels, kernel_call(): pl.pallas_call(body, in_specs=[VMEM] * len(args), out_specs=VMEM if singl...  7.45 us
    all_to_all x1, waiting for transfers between devices, per_device(): owned = lax.all_to_all(pack(query_grads[0]), 'layer', 0, 0, tiled=True)  2.91 us
    unnamed x6, local copies, waits for them, and re-layouts  2.46 us
  transfers between devices with their start and end apart: 25, of which 13 were waited for; matrix products, arithmetic and copies ran while one was open for 0% of the time, Pallas kernels for 17%

profile of v2, /device:TPU:24, one launch (start us, length us, event | category | flops | bytes accessed | tf_op | source)
XLA Modules:
  0.0 93.0 jit_solution(5116773718384745303)
XLA Ops:
  0.0 0.9 %copy-done = bf16[1,2,16,4096]{3,2,1,0:T(8,128)(2,1)S(1)} copy-done((bf16[1,2,16,4096]{3,2,1,0:T(8,128)(2,1)S(1)}, bf16[1,2,16,4096]{3,2,1,0:T(8,128)(2,1)}, u32[]{:S(2)}) %copy-start) | copy-done | bytes 262168
  1.0 1.2 %pack.1 = bf16[16,64,128]{2,1,0:T(8,128)(2,1)} custom-call(bf16[2,16,4096]{2,1,0:T(8,128)(2,1)S(1)} %bitcast.4), custom_call_target="tpu_custom_call" | custom-call | bytes 524288 | tf_op jit(solution)/shard_map/pack/pallas_call | solution.py:20
  2.1 11.3 %all-to-all-start = ((bf16[16,64,128]{2,1,0:T(8,128)(2,1)}), bf16[16,64,128]{2,1,0:T(8,128)(2,1)S(1)}, u32[]{:S(2)}, u32[]{:S(2)}) async-start(bf16[16,64,128]{2,1,0:T(8,128)(2,1)} %pack.1), calls=%async_computation | async-start | bytes 524288 | tf_op jit(solution)/shard_map/all_to_all | solution.py:362
  15.2 5.9 %power.1.refs_8_ = f32[12,128]{1,0:T(8,128)S(1)} custom-call(bf16[1536,4096]{1,0:T(8,128)(2,1)} %bitcast.7), custom_call_target="tpu_custom_call" | custom-call | flops 134217728 | bytes 13631488 | tf_op jit(solution)/shard_map/power/pallas_call | solution.py:194
  21.2 2.9 %all-to-all-done.x_ref = bf16[16,64,128]{2,1,0:T(8,128)(2,1)S(1)} async-done(((bf16[16,64,128]{2,1,0:T(8,128)(2,1)}), bf16[16,64,128]{2,1,0:T(8,128)(2,1)S(1)}, u32[]{:S(2)}, u32[]{:S(2)}) %all-to-all-start) | async-done | bytes 262176 | tf_op jit(solution)/shard_map/all_to_all | solution.py:362
  24.1 1.4 %ready.1.refs_0_ = bf16[32,4096]{1,0:T(8,128)(2,1)S(1)} custom-call(bf16[16,64,128]{2,1,0:T(8,128)(2,1)S(1)} %all-to-all-done.x_ref, bf16[64,256]{1,0:T(8,128)(2,1)S(1)} %get-tuple-element.35.left_ref, bf16[128,768]{1,0:T(8,128)(2,1)S(1)} %get-tuple-element.36.right_ref), custom_call_target="tpu_custom_call" | custom-call | flops 268435456 | bytes 524288 | tf_op jit(solution)/shard_map/ready/pallas_call | solution.py:20
  25.5 0.9 collective-permute-start.1
  26.4 1.5 %collective-permute-start.5 = (bf16[32,4096]{1,0:T(8,128)(2,1)S(1)}, bf16[32,4096]{1,0:T(8,128)(2,1)S(1)}, u32[]{:S(2)}, u32[]{:S(2)}) collective-permute-start(bf16[32,4096]{1,0:T(8,128)(2,1)S(1)} %ready.1.refs_0_), channel_id=1, source_target_pairs={{0,32},{1,33},{2,34},{3,35},{4,36},{5,37},{6,38},{7,39},{8,40},{9,... | collective-permute-start | bytes 786440 | tf_op jit(solution)/shard_map/ppermute | solution.py:46
  27.9 1.7 %collective-permute-start.6 = (bf16[32,4096]{1,0:T(8,128)(2,1)S(1)}, bf16[32,4096]{1,0:T(8,128)(2,1)S(1)}, u32[]{:S(2)}, u32[]{:S(2)}) collective-permute-start(bf16[32,4096]{1,0:T(8,128)(2,1)S(1)} %ready.1.refs_0_), channel_id=1, source_target_pairs={{0,96},{1,97},{2,98},{3,99},{4,100},{5,101},{6,102},{7,103},{8,104... | collective-permute-start | bytes 786440 | tf_op jit(solution)/shard_map/ppermute | solution.py:46
  29.7 1.8 %collective-permute-start = (bf16[32,4096]{1,0:T(8,128)(2,1)S(1)}, bf16[32,4096]{1,0:T(8,128)(2,1)S(1)}, u32[]{:S(2)}, u32[]{:S(2)}) collective-permute-start(bf16[32,4096]{1,0:T(8,128)(2,1)S(1)} %ready.1.refs_0_), channel_id=1, source_target_pairs={{0,64},{1,65},{2,66},{3,67},{4,68},{5,69},{6,70},{7,71},{8,72},{9,... | collective-permute-start | bytes 786440 | tf_op jit(solution)/shard_map/ppermute | solution.py:46
  32.0 2.0 %collective-permute-done.5.refs_1_ = bf16[32,4096]{1,0:T(8,128)(2,1)S(1)} collective-permute-done((bf16[32,4096]{1,0:T(8,128)(2,1)S(1)}, bf16[32,4096]{1,0:T(8,128)(2,1)S(1)}, u32[]{:S(2)}, u32[]{:S(2)}) %collective-permute-start.5) | collective-permute-done | bytes 262176 | tf_op jit(solution)/shard_map/ppermute | solution.py:46
  34.0 5.2 %collective-permute-done.6.refs_2_ = bf16[32,4096]{1,0:T(8,128)(2,1)S(1)} collective-permute-done((bf16[32,4096]{1,0:T(8,128)(2,1)S(1)}, bf16[32,4096]{1,0:T(8,128)(2,1)S(1)}, u32[]{:S(2)}, u32[]{:S(2)}) %collective-permute-start.6) | collective-permute-done | bytes 262176 | tf_op jit(solution)/shard_map/ppermute | solution.py:46
  39.2 1.4 %collective-permute-done.refs_0_ = bf16[32,4096]{1,0:T(8,128)(2,1)S(1)} collective-permute-done((bf16[32,4096]{1,0:T(8,128)(2,1)S(1)}, bf16[32,4096]{1,0:T(8,128)(2,1)S(1)}, u32[]{:S(2)}, u32[]{:S(2)}) %collective-permute-start) | collective-permute-done | bytes 262176 | tf_op jit(solution)/shard_map/ppermute | solution.py:46
  40.6 2.4 %collective-permute-start.3 = (bf16[32,4096]{1,0:T(8,128)(2,1)S(1)}, bf16[32,4096]{1,0:T(8,128)(2,1)S(1)}, u32[]{:S(2)}, u32[]{:S(2)}) collective-permute-start(bf16[32,4096]{1,0:T(8,128)(2,1)S(1)} %collective-permute-done.1.refs_3_), channel_id=1, source_target_pairs={{0,96},{1,97},{2,98},{3,99},{4,100},{5,101},{6,102},{7,103},{8,104... | collective-permute-start | bytes 786440 | tf_op jit(solution)/shard_map/ppermute | solution.py:46
  43.0 1.2 %collective-permute-start.4 = (bf16[32,4096]{1,0:T(8,128)(2,1)S(1)}, bf16[32,4096]{1,0:T(8,128)(2,1)S(1)}, u32[]{:S(2)}, u32[]{:S(2)}) collective-permute-start(bf16[32,4096]{1,0:T(8,128)(2,1)S(1)} %collective-permute-done.refs_0_), channel_id=1, source_target_pairs={{0,128},{1,129},{2,130},{3,131},{4,132},{5,133},{6,134},{7,135},{8... | collective-permute-start | bytes 786440 | tf_op jit(solution)/shard_map/ppermute | solution.py:46
  44.2 6.1 %first.1 = (bf16[2,32,1664]{2,1,0:T(8,128)(2,1)S(1)}, bf16[2,32,1664]{2,1,0:T(8,128)(2,1)S(1)}, bf16[2,32,1664]{2,1,0:T(8,128)(2,1)S(1)}, bf16[2,32,1664]{2,1,0:T(8,128)(2,1)S(1)}, bf16[1536,4096]{1,0:T(8,128)(2,1)S(1)}) custom-call(bf16[32,4096]{1,0:T(8,128)(2,1)S(1)} %ready.1.refs_0_, bf16[32,4096]{1,0:T(8,128)(2,1)S(1)} %collective-permute-done.5.refs_1_, ...), custom_call_target="tpu_custom_call" | custom-call | flops 3221225472 | bytes 13631488 | tf_op jit(solution)/shard_map/first/pallas_call | solution.py:194
  50.3 1.1 %collective-permute-done.4.refs_3_ = bf16[32,4096]{1,0:T(8,128)(2,1)S(1)} collective-permute-done((bf16[32,4096]{1,0:T(8,128)(2,1)S(1)}, bf16[32,4096]{1,0:T(8,128)(2,1)S(1)}, u32[]{:S(2)}, u32[]{:S(2)}) %collective-permute-start.4) | collective-permute-done | bytes 262176 | tf_op jit(solution)/shard_map/ppermute | solution.py:46
  52.4 1.9 %collective-permute-start.11 = (bf16[2,32,1664]{2,1,0:T(8,128)(2,1)S(1)}, bf16[2,32,1664]{2,1,0:T(8,128)(2,1)S(1)}, u32[]{:S(2)}, u32[]{:S(2)}) collective-permute-start(bf16[2,32,1664]{2,1,0:T(8,128)(2,1)S(1)} %get-tuple-element.43), channel_id=1, source_target_pairs={{0,1},{1,2},{2,3},{3,0},{4,5},{5,6},{6,7},{7,4},{8,9},{9,10},{10,1... | collective-permute-start | bytes 638984 | tf_op jit(solution)/shard_map/ppermute | solution.py:46
  54.4 1.3 %collective-permute-start.12 = (bf16[2,32,1664]{2,1,0:T(8,128)(2,1)S(1)}, bf16[2,32,1664]{2,1,0:T(8,128)(2,1)S(1)}, u32[]{:S(2)}, u32[]{:S(2)}) collective-permute-start(bf16[2,32,1664]{2,1,0:T(8,128)(2,1)S(1)} %get-tuple-element.44), channel_id=1, source_target_pairs={{0,2},{1,3},{2,0},{3,1},{4,6},{5,7},{6,4},{7,5},{8,10},{9,11},{10,... | collective-permute-start | bytes 638984 | tf_op jit(solution)/shard_map/ppermute | solution.py:46
  55.7 3.5 %second.1 = (bf16[2,32,1536]{2,1,0:T(8,128)(2,1)S(1)}, bf16[2,32,1536]{2,1,0:T(8,128)(2,1)S(1)}, bf16[2,32,1536]{2,1,0:T(8,128)(2,1)S(1)}, bf16[2,32,1536]{2,1,0:T(8,128)(2,1)S(1)}) custom-call(bf16[32,4096]{1,0:T(8,128)(2,1)S(1)} %collective-permute-done.refs_0_, bf16[32,4096]{1,0:T(8,128)(2,1)S(1)} %collective-permute-done.2.refs_1_, ...), custom_call_target="tpu_custom_call" | custom-call | flops 3221225472 | bytes 15728640 | tf_op jit(solution)/shard_map/second/pallas_call | solution.py:20
  59.3 3.2 %collective-permute-start.18 = (bf16[2,32,1536]{2,1,0:T(8,128)(2,1)S(1)}, bf16[2,32,1536]{2,1,0:T(8,128)(2,1)S(1)}, u32[]{:S(2)}, u32[]{:S(2)}) collective-permute-start(bf16[2,32,1536]{2,1,0:T(8,128)(2,1)S(1)} %get-tuple-element.52), channel_id=1, source_target_pairs={{0,1},{1,2},{2,3},{3,0},{4,5},{5,6},{6,7},{7,4},{8,9},{9,10},{10,1... | collective-permute-start | bytes 589832 | tf_op jit(solution)/shard_map/ppermute | solution.py:46
  62.5 1.0 %collective-permute-start.19 = (bf16[2,32,1536]{2,1,0:T(8,128)(2,1)S(1)}, bf16[2,32,1536]{2,1,0:T(8,128)(2,1)S(1)}, u32[]{:S(2)}, u32[]{:S(2)}) collective-permute-start(bf16[2,32,1536]{2,1,0:T(8,128)(2,1)S(1)} %get-tuple-element.53), channel_id=1, source_target_pairs={{0,2},{1,3},{2,0},{3,1},{4,6},{5,7},{6,4},{7,5},{8,10},{9,11},{10,... | collective-permute-start | bytes 589832 | tf_op jit(solution)/shard_map/ppermute | solution.py:46
  64.1 4.6 %collective-permute-done.13.refs_3_ = bf16[2,32,1664]{2,1,0:T(8,128)(2,1)S(1)} collective-permute-done((bf16[2,32,1664]{2,1,0:T(8,128)(2,1)S(1)}, bf16[2,32,1664]{2,1,0:T(8,128)(2,1)S(1)}, u32[]{:S(2)}, u32[]{:S(2)}) %collective-permute-start.13) | collective-permute-done | bytes 213024 | tf_op jit(solution)/shard_map/ppermute | solution.py:46
  68.7 3.4 %collective-permute-done.18.refs_5_ = bf16[2,32,1536]{2,1,0:T(8,128)(2,1)S(1)} collective-permute-done((bf16[2,32,1536]{2,1,0:T(8,128)(2,1)S(1)}, bf16[2,32,1536]{2,1,0:T(8,128)(2,1)S(1)}, u32[]{:S(2)}, u32[]{:S(2)}) %collective-permute-start.18) | collective-permute-done | bytes 196640 | tf_op jit(solution)/shard_map/ppermute | solution.py:46
  72.1 0.8 collective-permute-done.19.refs_6_
  72.9 2.8 %collective-permute-done.20.refs_7_ = bf16[2,32,1536]{2,1,0:T(8,128)(2,1)S(1)} collective-permute-done((bf16[2,32,1536]{2,1,0:T(8,128)(2,1)S(1)}, bf16[2,32,1536]{2,1,0:T(8,128)(2,1)S(1)}, u32[]{:S(2)}, u32[]{:S(2)}) %collective-permute-start.20) | collective-permute-done | bytes 196640 | tf_op jit(solution)/shard_map/ppermute | solution.py:46
  76.1 1.6 %collective-permute-start.21 = (bf16[32,1664]{1,0:T(8,128)(2,1)S(1)}, bf16[32,1664]{1,0:T(8,128)(2,1)S(1)}, u32[]{:S(2)}, u32[]{:S(2)}) collective-permute-start(bf16[32,1664]{1,0:T(8,128)(2,1)S(1)} %get-tuple-element.56), channel_id=1, source_target_pairs={{0,4},{1,5},{2,6},{3,7},{4,8},{5,9},{6,10},{7,11},{8,12},{9,13},{1... | collective-permute-start | bytes 319496 | tf_op jit(solution)/shard_map/ppermute | solution.py:46
  77.7 2.6 %collective-permute-start.22 = (bf16[32,1664]{1,0:T(8,128)(2,1)S(1)}, bf16[32,1664]{1,0:T(8,128)(2,1)S(1)}, u32[]{:S(2)}, u32[]{:S(2)}) collective-permute-start(bf16[32,1664]{1,0:T(8,128)(2,1)S(1)} %get-tuple-element.57), channel_id=1, source_target_pairs={{0,8},{1,9},{2,10},{3,11},{4,12},{5,13},{6,14},{7,15},{8,0},{9,1},... | collective-permute-start | bytes 319496 | tf_op jit(solution)/shard_map/ppermute | solution.py:46
  80.3 2.2 %collective-permute-start.23 = (bf16[32,1664]{1,0:T(8,128)(2,1)S(1)}, bf16[32,1664]{1,0:T(8,128)(2,1)S(1)}, u32[]{:S(2)}, u32[]{:S(2)}) collective-permute-start(bf16[32,1664]{1,0:T(8,128)(2,1)S(1)} %get-tuple-element.58), channel_id=1, source_target_pairs={{0,12},{1,13},{2,14},{3,15},{4,0},{5,1},{6,2},{7,3},{8,4},{9,5},{1... | collective-permute-start | bytes 319496 | tf_op jit(solution)/shard_map/ppermute | solution.py:46
  82.5 5.6 %collective-permute-done.21.a = bf16[32,1664]{1,0:T(8,128)(2,1)S(1)} collective-permute-done((bf16[32,1664]{1,0:T(8,128)(2,1)S(1)}, bf16[32,1664]{1,0:T(8,128)(2,1)S(1)}, u32[]{:S(2)}, u32[]{:S(2)}) %collective-permute-start.21) | collective-permute-done | bytes 106528 | tf_op jit(solution)/shard_map/ppermute | solution.py:46
  88.1 4.2 %collective-permute-done.23.c = bf16[32,1664]{1,0:T(8,128)(2,1)S(1)} collective-permute-done((bf16[32,1664]{1,0:T(8,128)(2,1)S(1)}, bf16[32,1664]{1,0:T(8,128)(2,1)S(1)}, u32[]{:S(2)}, u32[]{:S(2)}) %collective-permute-start.23) | collective-permute-done | bytes 106528 | tf_op jit(solution)/shard_map/ppermute | solution.py:46
  92.3 0.8 finish.1
  (32 shorter events, 4.3 us)
Async XLA Ops:
  0.0 0.9 %copy-start = (bf16[1,2,16,4096]{3,2,1,0:T(8,128)(2,1)S(1)}, bf16[1,2,16,4096]{3,2,1,0:T(8,128)(2,1)}, u32[]{:S(2)}) copy-start(bf16[1,2,16,4096]{3,2,1,0:T(8,128)(2,1)} %param.4) | copy-start | bytes 786436
  2.1 22.0 %all-to-all-start = ((bf16[16,64,128]{2,1,0:T(8,128)(2,1)}), bf16[16,64,128]{2,1,0:T(8,128)(2,1)S(1)}, u32[]{:S(2)}, u32[]{:S(2)}) async-start(bf16[16,64,128]{2,1,0:T(8,128)(2,1)} %pack.1), calls=%async_computation | async-start | bytes 524288 | tf_op jit(solution)/shard_map/all_to_all | solution.py:362
  13.4 0.8 copy-start.1
  14.2 0.8 copy-start.2
  25.5 6.5 %collective-permute-start.1 = (bf16[32,4096]{1,0:T(8,128)(2,1)S(1)}, bf16[32,4096]{1,0:T(8,128)(2,1)S(1)}, u32[]{:S(2)}, u32[]{:S(2)}) collective-permute-start(bf16[32,4096]{1,0:T(8,128)(2,1)S(1)} %ready.1.refs_0_), channel_id=1, source_target_pairs={{0,128},{1,129},{2,130},{3,131},{4,132},{5,133},{6,134},{7,135},{8... | collective-permute-start | bytes 786440 | tf_op jit(solution)/shard_map/ppermute | solution.py:46
  26.4 7.6 %collective-permute-start.5 = (bf16[32,4096]{1,0:T(8,128)(2,1)S(1)}, bf16[32,4096]{1,0:T(8,128)(2,1)S(1)}, u32[]{:S(2)}, u32[]{:S(2)}) collective-permute-start(bf16[32,4096]{1,0:T(8,128)(2,1)S(1)} %ready.1.refs_0_), channel_id=1, source_target_pairs={{0,32},{1,33},{2,34},{3,35},{4,36},{5,37},{6,38},{7,39},{8,40},{9,... | collective-permute-start | bytes 786440 | tf_op jit(solution)/shard_map/ppermute | solution.py:46
  27.9 11.3 %collective-permute-start.6 = (bf16[32,4096]{1,0:T(8,128)(2,1)S(1)}, bf16[32,4096]{1,0:T(8,128)(2,1)S(1)}, u32[]{:S(2)}, u32[]{:S(2)}) collective-permute-start(bf16[32,4096]{1,0:T(8,128)(2,1)S(1)} %ready.1.refs_0_), channel_id=1, source_target_pairs={{0,96},{1,97},{2,98},{3,99},{4,100},{5,101},{6,102},{7,103},{8,104... | collective-permute-start | bytes 786440 | tf_op jit(solution)/shard_map/ppermute | solution.py:46
  29.7 9.5 %collective-permute-start.7 = (bf16[32,4096]{1,0:T(8,128)(2,1)S(1)}, bf16[32,4096]{1,0:T(8,128)(2,1)S(1)}, u32[]{:S(2)}, u32[]{:S(2)}) collective-permute-start(bf16[32,4096]{1,0:T(8,128)(2,1)S(1)} %ready.1.refs_0_), channel_id=1, source_target_pairs={{0,16},{1,17},{2,18},{3,19},{4,20},{5,21},{6,22},{7,23},{8,24},{9,... | collective-permute-start | bytes 786440 | tf_op jit(solution)/shard_map/ppermute | solution.py:46
  29.7 10.9 %collective-permute-start = (bf16[32,4096]{1,0:T(8,128)(2,1)S(1)}, bf16[32,4096]{1,0:T(8,128)(2,1)S(1)}, u32[]{:S(2)}, u32[]{:S(2)}) collective-permute-start(bf16[32,4096]{1,0:T(8,128)(2,1)S(1)} %ready.1.refs_0_), channel_id=1, source_target_pairs={{0,64},{1,65},{2,66},{3,67},{4,68},{5,69},{6,70},{7,71},{8,72},{9,... | collective-permute-start | bytes 786440 | tf_op jit(solution)/shard_map/ppermute | solution.py:46
  32.0 11.0 %collective-permute-start.10 = (bf16[32,4096]{1,0:T(8,128)(2,1)S(1)}, bf16[32,4096]{1,0:T(8,128)(2,1)S(1)}, u32[]{:S(2)}, u32[]{:S(2)}) collective-permute-start(bf16[32,4096]{1,0:T(8,128)(2,1)S(1)} %collective-permute-done.1.refs_3_), channel_id=1, source_target_pairs={{0,16},{1,17},{2,18},{3,19},{4,20},{5,21},{6,22},{7,23},{8,24},{9,... | collective-permute-start | bytes 786440 | tf_op jit(solution)/shard_map/ppermute | solution.py:46
  34.0 10.2 %collective-permute-start.8 = (bf16[32,4096]{1,0:T(8,128)(2,1)S(1)}, bf16[32,4096]{1,0:T(8,128)(2,1)S(1)}, u32[]{:S(2)}, u32[]{:S(2)}) collective-permute-start(bf16[32,4096]{1,0:T(8,128)(2,1)S(1)} %collective-permute-done.5.refs_1_), channel_id=1, source_target_pairs={{0,16},{1,17},{2,18},{3,19},{4,20},{5,21},{6,22},{7,23},{8,24},{9,... | collective-permute-start | bytes 786440 | tf_op jit(solution)/shard_map/ppermute | solution.py:46
  39.2 5.0 %collective-permute-start.9 = (bf16[32,4096]{1,0:T(8,128)(2,1)S(1)}, bf16[32,4096]{1,0:T(8,128)(2,1)S(1)}, u32[]{:S(2)}, u32[]{:S(2)}) collective-permute-start(bf16[32,4096]{1,0:T(8,128)(2,1)S(1)} %collective-permute-done.6.refs_2_), channel_id=1, source_target_pairs={{0,16},{1,17},{2,18},{3,19},{4,20},{5,21},{6,22},{7,23},{8,24},{9,... | collective-permute-start | bytes 786440 | tf_op jit(solution)/shard_map/ppermute | solution.py:46
  39.2 11.1 %collective-permute-start.2 = (bf16[32,4096]{1,0:T(8,128)(2,1)S(1)}, bf16[32,4096]{1,0:T(8,128)(2,1)S(1)}, u32[]{:S(2)}, u32[]{:S(2)}) collective-permute-start(bf16[32,4096]{1,0:T(8,128)(2,1)S(1)} %collective-permute-done.1.refs_3_), channel_id=1, source_target_pairs={{0,32},{1,33},{2,34},{3,35},{4,36},{5,37},{6,38},{7,39},{8,40},{9,... | collective-permute-start | bytes 786440 | tf_op jit(solution)/shard_map/ppermute | solution.py:46
  40.6 9.7 %collective-permute-start.3 = (bf16[32,4096]{1,0:T(8,128)(2,1)S(1)}, bf16[32,4096]{1,0:T(8,128)(2,1)S(1)}, u32[]{:S(2)}, u32[]{:S(2)}) collective-permute-start(bf16[32,4096]{1,0:T(8,128)(2,1)S(1)} %collective-permute-done.1.refs_3_), channel_id=1, source_target_pairs={{0,96},{1,97},{2,98},{3,99},{4,100},{5,101},{6,102},{7,103},{8,104... | collective-permute-start | bytes 786440 | tf_op jit(solution)/shard_map/ppermute | solution.py:46
  43.0 8.4 %collective-permute-start.4 = (bf16[32,4096]{1,0:T(8,128)(2,1)S(1)}, bf16[32,4096]{1,0:T(8,128)(2,1)S(1)}, u32[]{:S(2)}, u32[]{:S(2)}) collective-permute-start(bf16[32,4096]{1,0:T(8,128)(2,1)S(1)} %collective-permute-done.refs_0_), channel_id=1, source_target_pairs={{0,128},{1,129},{2,130},{3,131},{4,132},{5,133},{6,134},{7,135},{8... | collective-permute-start | bytes 786440 | tf_op jit(solution)/shard_map/ppermute | solution.py:46
  51.4 3.0 %collective-permute-start.14 = (bf16[32,4096]{1,0:T(8,128)(2,1)S(1)}, bf16[32,4096]{1,0:T(8,128)(2,1)S(1)}, u32[]{:S(2)}, u32[]{:S(2)}) collective-permute-start(bf16[32,4096]{1,0:T(8,128)(2,1)S(1)} %collective-permute-done.refs_0_), channel_id=1, source_target_pairs={{0,16},{1,17},{2,18},{3,19},{4,20},{5,21},{6,22},{7,23},{8,24},{9,... | collective-permute-start | bytes 786440 | tf_op jit(solution)/shard_map/ppermute | solution.py:46
  51.4 4.3 %collective-permute-start.15 = (bf16[32,4096]{1,0:T(8,128)(2,1)S(1)}, bf16[32,4096]{1,0:T(8,128)(2,1)S(1)}, u32[]{:S(2)}, u32[]{:S(2)}) collective-permute-start(bf16[32,4096]{1,0:T(8,128)(2,1)S(1)} %collective-permute-done.2.refs_1_), channel_id=1, source_target_pairs={{0,16},{1,17},{2,18},{3,19},{4,20},{5,21},{6,22},{7,23},{8,24},{9,... | collective-permute-start | bytes 786440 | tf_op jit(solution)/shard_map/ppermute | solution.py:46
  51.9 3.8 %collective-permute-start.16 = (bf16[32,4096]{1,0:T(8,128)(2,1)S(1)}, bf16[32,4096]{1,0:T(8,128)(2,1)S(1)}, u32[]{:S(2)}, u32[]{:S(2)}) collective-permute-start(bf16[32,4096]{1,0:T(8,128)(2,1)S(1)} %collective-permute-done.3.refs_2_), channel_id=1, source_target_pairs={{0,16},{1,17},{2,18},{3,19},{4,20},{5,21},{6,22},{7,23},{8,24},{9,... | collective-permute-start | bytes 786440 | tf_op jit(solution)/shard_map/ppermute | solution.py:46
  51.9 3.8 %collective-permute-start.17 = (bf16[32,4096]{1,0:T(8,128)(2,1)S(1)}, bf16[32,4096]{1,0:T(8,128)(2,1)S(1)}, u32[]{:S(2)}, u32[]{:S(2)}) collective-permute-start(bf16[32,4096]{1,0:T(8,128)(2,1)S(1)} %collective-permute-done.4.refs_3_), channel_id=1, source_target_pairs={{0,16},{1,17},{2,18},{3,19},{4,20},{5,21},{6,22},{7,23},{8,24},{9,... | collective-permute-start | bytes 786440 | tf_op jit(solution)/shard_map/ppermute | solution.py:46
  52.4 11.1 %collective-permute-start.11 = (bf16[2,32,1664]{2,1,0:T(8,128)(2,1)S(1)}, bf16[2,32,1664]{2,1,0:T(8,128)(2,1)S(1)}, u32[]{:S(2)}, u32[]{:S(2)}) collective-permute-start(bf16[2,32,1664]{2,1,0:T(8,128)(2,1)S(1)} %get-tuple-element.43), channel_id=1, source_target_pairs={{0,1},{1,2},{2,3},{3,0},{4,5},{5,6},{6,7},{7,4},{8,9},{9,10},{10,1... | collective-permute-start | bytes 638984 | tf_op jit(solution)/shard_map/ppermute | solution.py:46
  54.4 9.7 %collective-permute-start.12 = (bf16[2,32,1664]{2,1,0:T(8,128)(2,1)S(1)}, bf16[2,32,1664]{2,1,0:T(8,128)(2,1)S(1)}, u32[]{:S(2)}, u32[]{:S(2)}) collective-permute-start(bf16[2,32,1664]{2,1,0:T(8,128)(2,1)S(1)} %get-tuple-element.44), channel_id=1, source_target_pairs={{0,2},{1,3},{2,0},{3,1},{4,6},{5,7},{6,4},{7,5},{8,10},{9,11},{10,... | collective-permute-start | bytes 638984 | tf_op jit(solution)/shard_map/ppermute | solution.py:46
  55.7 13.0 %collective-permute-start.13 = (bf16[2,32,1664]{2,1,0:T(8,128)(2,1)S(1)}, bf16[2,32,1664]{2,1,0:T(8,128)(2,1)S(1)}, u32[]{:S(2)}, u32[]{:S(2)}) collective-permute-start(bf16[2,32,1664]{2,1,0:T(8,128)(2,1)S(1)} %get-tuple-element.45), channel_id=1, source_target_pairs={{0,3},{1,0},{2,1},{3,2},{4,7},{5,4},{6,5},{7,6},{8,11},{9,8},{10,9... | collective-permute-start | bytes 638984 | tf_op jit(solution)/shard_map/ppermute | solution.py:46
  59.3 12.8 %collective-permute-start.18 = (bf16[2,32,1536]{2,1,0:T(8,128)(2,1)S(1)}, bf16[2,32,1536]{2,1,0:T(8,128)(2,1)S(1)}, u32[]{:S(2)}, u32[]{:S(2)}) collective-permute-start(bf16[2,32,1536]{2,1,0:T(8,128)(2,1)S(1)} %get-tuple-element.52), channel_id=1, source_target_pairs={{0,1},{1,2},{2,3},{3,0},{4,5},{5,6},{6,7},{7,4},{8,9},{9,10},{10,1... | collective-permute-start | bytes 589832 | tf_op jit(solution)/shard_map/ppermute | solution.py:46
  62.5 10.4 %collective-permute-start.19 = (bf16[2,32,1536]{2,1,0:T(8,128)(2,1)S(1)}, bf16[2,32,1536]{2,1,0:T(8,128)(2,1)S(1)}, u32[]{:S(2)}, u32[]{:S(2)}) collective-permute-start(bf16[2,32,1536]{2,1,0:T(8,128)(2,1)S(1)} %get-tuple-element.53), channel_id=1, source_target_pairs={{0,2},{1,3},{2,0},{3,1},{4,6},{5,7},{6,4},{7,5},{8,10},{9,11},{10,... | collective-permute-start | bytes 589832 | tf_op jit(solution)/shard_map/ppermute | solution.py:46
  63.5 12.2 %collective-permute-start.20 = (bf16[2,32,1536]{2,1,0:T(8,128)(2,1)S(1)}, bf16[2,32,1536]{2,1,0:T(8,128)(2,1)S(1)}, u32[]{:S(2)}, u32[]{:S(2)}) collective-permute-start(bf16[2,32,1536]{2,1,0:T(8,128)(2,1)S(1)} %get-tuple-element.54), channel_id=1, source_target_pairs={{0,3},{1,0},{2,1},{3,2},{4,7},{5,4},{6,5},{7,6},{8,11},{9,8},{10,9... | collective-permute-start | bytes 589832 | tf_op jit(solution)/shard_map/ppermute | solution.py:46
  76.1 12.0 %collective-permute-start.21 = (bf16[32,1664]{1,0:T(8,128)(2,1)S(1)}, bf16[32,1664]{1,0:T(8,128)(2,1)S(1)}, u32[]{:S(2)}, u32[]{:S(2)}) collective-permute-start(bf16[32,1664]{1,0:T(8,128)(2,1)S(1)} %get-tuple-element.56), channel_id=1, source_target_pairs={{0,4},{1,5},{2,6},{3,7},{4,8},{5,9},{6,10},{7,11},{8,12},{9,13},{1... | collective-permute-start | bytes 319496 | tf_op jit(solution)/shard_map/ppermute | solution.py:46
  77.7 10.4 %collective-permute-start.22 = (bf16[32,1664]{1,0:T(8,128)(2,1)S(1)}, bf16[32,1664]{1,0:T(8,128)(2,1)S(1)}, u32[]{:S(2)}, u32[]{:S(2)}) collective-permute-start(bf16[32,1664]{1,0:T(8,128)(2,1)S(1)} %get-tuple-element.57), channel_id=1, source_target_pairs={{0,8},{1,9},{2,10},{3,11},{4,12},{5,13},{6,14},{7,15},{8,0},{9,1},... | collective-permute-start | bytes 319496 | tf_op jit(solution)/shard_map/ppermute | solution.py:46
  80.3 12.0 %collective-permute-start.23 = (bf16[32,1664]{1,0:T(8,128)(2,1)S(1)}, bf16[32,1664]{1,0:T(8,128)(2,1)S(1)}, u32[]{:S(2)}, u32[]{:S(2)}) collective-permute-start(bf16[32,1664]{1,0:T(8,128)(2,1)S(1)} %get-tuple-element.58), channel_id=1, source_target_pairs={{0,12},{1,13},{2,14},{3,15},{4,0},{5,1},{6,2},{7,3},{8,4},{9,5},{1... | collective-permute-start | bytes 319496 | tf_op jit(solution)/shard_map/ppermute | solution.py:46

commit v3 on v2

--- a/solution.py
+++ b/solution.py
@@ -369,8 +369,10 @@
     pieces = {(0, 0): own, (1, 0): other, (0, 1): shifted(own, x=1), (0, 3): shifted(own, x=3)}
     pieces[0, 2] = shifted(own, x=2)
     pieces[1, 1], pieces[1, 3] = shifted(other, x=1), shifted(other, x=3)
+
+    arrived = (pieces[0, 1], pieces[0, 3], pieces[0, 2])
+    pieces[0, 1], pieces[0, 3], pieces[0, 2] = lax.optimization_barrier(arrived)
     pieces[1, 2] = shifted(pieces[0, 2], zl=1)
-
     mine = [pieces[chunk] for chunk in HALVES[0]]
     mine += [shifted(piece, c=1) for piece in mine]
     chunks = [(a, k, e) for e in (0, 1) for a, k in HALVES[0]]

time: 93.4 us -> 92.8 us (level)
  waiting for transfers between devices: 35 us -> 31.3 us
  starting transfers between devices: 35.9 us -> 38.5 us
    ppermute x24, waiting for transfers between devices: 32.1 us -> 28.4 us  [shifted(): return lax.ppermute(value, ('dp', 'layer'), pairs)]
    ppermute x24, starting transfers between devices: 24.6 us -> 27.2 us  [shifted(): return lax.ppermute(value, ('dp', 'layer'), pairs)]
  transfers between devices with their start and end apart: 25 -> 25, of which waited for: 13 -> 11; matrix products, arithmetic and copies ran while one was open for 0% -> 0% of each run, Pallas kernels for 17% -> 17%
where the time goes in v3:
time: 92.8 us; the launch traced here: 91.8 us
  starting transfers between devices  38.5 us (41%)
  waiting for transfers between devices  31.3 us (34%)
  Pallas kernels  19.5 us (21%)
  local copies, waits for them, and re-layouts  2.46 us (3%)
    ppermute x24, waiting for transfers between devices, shifted(): return lax.ppermute(value, ('dp', 'layer'), pairs)  28.4 us
    ppermute x24, starting transfers between devices, shifted(): return lax.ppermute(value, ('dp', 'layer'), pairs)  27.2 us
    pallas_call x2, Pallas kernels, corpus_call(): pl.pallas_call(body, in_specs=[VMEM] * (len(args) - 1) + [pl.BlockSpec(me...  12 us
    all_to_all x1, starting transfers between devices, per_device(): owned = lax.all_to_all(pack(query_grads[0]), 'layer', 0, 0, tiled=True)  11.3 us
    pallas_call x6, Pallas kernels, kernel_call(): pl.pallas_call(body, in_specs=[VMEM] * len(args), out_specs=VMEM if singl...  7.45 us
    all_to_all x1, waiting for transfers between devices, per_device(): owned = lax.all_to_all(pack(query_grads[0]), 'layer', 0, 0, tiled=True)  2.91 us
    unnamed x6, local copies, waits for them, and re-layouts  2.46 us
  transfers between devices with their start and end apart: 25, of which 11 were waited for; matrix products, arithmetic and copies ran while one was open for 0% of the time, Pallas kernels for 17%

profile of v3, /device:TPU:24, one launch (start us, length us, event | category | flops | bytes accessed | tf_op | source)
XLA Modules:
  0.0 91.8 jit_solution(3597118120731547686)
XLA Ops:
  0.0 0.9 %copy-done = bf16[1,2,16,4096]{3,2,1,0:T(8,128)(2,1)S(1)} copy-done((bf16[1,2,16,4096]{3,2,1,0:T(8,128)(2,1)S(1)}, bf16[1,2,16,4096]{3,2,1,0:T(8,128)(2,1)}, u32[]{:S(2)}) %copy-start) | copy-done | bytes 262168
  1.0 1.2 %pack.1 = bf16[16,64,128]{2,1,0:T(8,128)(2,1)} custom-call(bf16[2,16,4096]{2,1,0:T(8,128)(2,1)S(1)} %bitcast.4), custom_call_target="tpu_custom_call" | custom-call | bytes 524288 | tf_op jit(solution)/shard_map/pack/pallas_call | solution.py:20
  2.1 11.3 %all-to-all-start = ((bf16[16,64,128]{2,1,0:T(8,128)(2,1)}), bf16[16,64,128]{2,1,0:T(8,128)(2,1)S(1)}, u32[]{:S(2)}, u32[]{:S(2)}) async-start(bf16[16,64,128]{2,1,0:T(8,128)(2,1)} %pack.1), calls=%async_computation | async-start | bytes 524288 | tf_op jit(solution)/shard_map/all_to_all | solution.py:362
  14.2 0.8 copy-done.2
  15.2 5.9 %power.1.refs_8_ = f32[12,128]{1,0:T(8,128)S(1)} custom-call(bf16[1536,4096]{1,0:T(8,128)(2,1)} %bitcast.7), custom_call_target="tpu_custom_call" | custom-call | flops 134217728 | bytes 13631488 | tf_op jit(solution)/shard_map/power/pallas_call | solution.py:194
  21.2 2.9 %all-to-all-done.x_ref = bf16[16,64,128]{2,1,0:T(8,128)(2,1)S(1)} async-done(((bf16[16,64,128]{2,1,0:T(8,128)(2,1)}), bf16[16,64,128]{2,1,0:T(8,128)(2,1)S(1)}, u32[]{:S(2)}, u32[]{:S(2)}) %all-to-all-start) | async-done | bytes 262176 | tf_op jit(solution)/shard_map/all_to_all | solution.py:362
  24.1 1.4 %ready.1.refs_0_ = bf16[32,4096]{1,0:T(8,128)(2,1)S(1)} custom-call(bf16[16,64,128]{2,1,0:T(8,128)(2,1)S(1)} %all-to-all-done.x_ref, bf16[64,256]{1,0:T(8,128)(2,1)S(1)} %get-tuple-element.38.left_ref, bf16[128,768]{1,0:T(8,128)(2,1)S(1)} %get-tuple-element.39.right_ref), custom_call_target="tpu_custom_call" | custom-call | flops 268435456 | bytes 524288 | tf_op jit(solution)/shard_map/ready/pallas_call | solution.py:20
  25.5 1.6 %collective-permute-start = (bf16[32,4096]{1,0:T(8,128)(2,1)S(1)}, bf16[32,4096]{1,0:T(8,128)(2,1)S(1)}, u32[]{:S(2)}, u32[]{:S(2)}) collective-permute-start(bf16[32,4096]{1,0:T(8,128)(2,1)S(1)} %ready.1.refs_0_), channel_id=1, source_target_pairs={{0,32},{1,33},{2,34},{3,35},{4,36},{5,37},{6,38},{7,39},{8,40},{9,... | collective-permute-start | bytes 786440 | tf_op jit(solution)/shard_map/ppermute | solution.py:46
  27.1 1.7 %collective-permute-start.1 = (bf16[32,4096]{1,0:T(8,128)(2,1)S(1)}, bf16[32,4096]{1,0:T(8,128)(2,1)S(1)}, u32[]{:S(2)}, u32[]{:S(2)}) collective-permute-start(bf16[32,4096]{1,0:T(8,128)(2,1)S(1)} %ready.1.refs_0_), channel_id=1, source_target_pairs={{0,96},{1,97},{2,98},{3,99},{4,100},{5,101},{6,102},{7,103},{8,104... | collective-permute-start | bytes 786440 | tf_op jit(solution)/shard_map/ppermute | solution.py:46
  28.8 1.8 %collective-permute-start.2 = (bf16[32,4096]{1,0:T(8,128)(2,1)S(1)}, bf16[32,4096]{1,0:T(8,128)(2,1)S(1)}, u32[]{:S(2)}, u32[]{:S(2)}) collective-permute-start(bf16[32,4096]{1,0:T(8,128)(2,1)S(1)} %ready.1.refs_0_), channel_id=1, source_target_pairs={{0,64},{1,65},{2,66},{3,67},{4,68},{5,69},{6,70},{7,71},{8,72},{9,... | collective-permute-start | bytes 786440 | tf_op jit(solution)/shard_map/ppermute | solution.py:46
  30.6 0.8 collective-permute-start.3
  31.5 4.5 %collective-permute-done.refs_1_ = bf16[32,4096]{1,0:T(8,128)(2,1)S(1)} collective-permute-done((bf16[32,4096]{1,0:T(8,128)(2,1)S(1)}, bf16[32,4096]{1,0:T(8,128)(2,1)S(1)}, u32[]{:S(2)}, u32[]{:S(2)}) %collective-permute-start) | collective-permute-done | bytes 262176 | tf_op jit(solution)/shard_map/ppermute | solution.py:46
  36.0 2.9 %collective-permute-done.2.refs_0_ = bf16[32,4096]{1,0:T(8,128)(2,1)S(1)} collective-permute-done((bf16[32,4096]{1,0:T(8,128)(2,1)S(1)}, bf16[32,4096]{1,0:T(8,128)(2,1)S(1)}, u32[]{:S(2)}, u32[]{:S(2)}) %collective-permute-start.2) | collective-permute-done | bytes 262176 | tf_op jit(solution)/shard_map/ppermute | solution.py:46
  39.4 0.8 collective-permute-start.6
  40.2 1.1 %collective-permute-start.4 = (bf16[32,4096]{1,0:T(8,128)(2,1)S(1)}, bf16[32,4096]{1,0:T(8,128)(2,1)S(1)}, u32[]{:S(2)}, u32[]{:S(2)}) collective-permute-start(bf16[32,4096]{1,0:T(8,128)(2,1)S(1)} %collective-permute-done.3.refs_3_), channel_id=1, source_target_pairs={{0,32},{1,33},{2,34},{3,35},{4,36},{5,37},{6,38},{7,39},{8,40},{9,... | collective-permute-start | bytes 786440 | tf_op jit(solution)/shard_map/ppermute | solution.py:46
  41.3 2.1 %collective-permute-start.5 = (bf16[32,4096]{1,0:T(8,128)(2,1)S(1)}, bf16[32,4096]{1,0:T(8,128)(2,1)S(1)}, u32[]{:S(2)}, u32[]{:S(2)}) collective-permute-start(bf16[32,4096]{1,0:T(8,128)(2,1)S(1)} %collective-permute-done.3.refs_3_), channel_id=1, source_target_pairs={{0,96},{1,97},{2,98},{3,99},{4,100},{5,101},{6,102},{7,103},{8,104... | collective-permute-start | bytes 786440 | tf_op jit(solution)/shard_map/ppermute | solution.py:46
  43.5 6.1 %first.1 = (bf16[2,32,1664]{2,1,0:T(8,128)(2,1)S(1)}, bf16[2,32,1664]{2,1,0:T(8,128)(2,1)S(1)}, bf16[2,32,1664]{2,1,0:T(8,128)(2,1)S(1)}, bf16[2,32,1664]{2,1,0:T(8,128)(2,1)S(1)}, bf16[1536,4096]{1,0:T(8,128)(2,1)S(1)}) custom-call(bf16[32,4096]{1,0:T(8,128)(2,1)S(1)} %ready.1.refs_0_, bf16[32,4096]{1,0:T(8,128)(2,1)S(1)} %collective-permute-done.refs_1_, ...), custom_call_target="tpu_custom_call" | custom-call | flops 3221225472 | bytes 13631488 | tf_op jit(solution)/shard_map/first/pallas_call | solution.py:194
  50.9 1.8 %collective-permute-start.11 = (bf16[2,32,1664]{2,1,0:T(8,128)(2,1)S(1)}, bf16[2,32,1664]{2,1,0:T(8,128)(2,1)S(1)}, u32[]{:S(2)}, u32[]{:S(2)}) collective-permute-start(bf16[2,32,1664]{2,1,0:T(8,128)(2,1)S(1)} %get-tuple-element.49), channel_id=1, source_target_pairs={{0,1},{1,2},{2,3},{3,0},{4,5},{5,6},{6,7},{7,4},{8,9},{9,10},{10,1... | collective-permute-start | bytes 638984 | tf_op jit(solution)/shard_map/ppermute | solution.py:46
  52.7 1.1 %collective-permute-start.12 = (bf16[2,32,1664]{2,1,0:T(8,128)(2,1)S(1)}, bf16[2,32,1664]{2,1,0:T(8,128)(2,1)S(1)}, u32[]{:S(2)}, u32[]{:S(2)}) collective-permute-start(bf16[2,32,1664]{2,1,0:T(8,128)(2,1)S(1)} %get-tuple-element.50), channel_id=1, source_target_pairs={{0,2},{1,3},{2,0},{3,1},{4,6},{5,7},{6,4},{7,5},{8,10},{9,11},{10,... | collective-permute-start | bytes 638984 | tf_op jit(solution)/shard_map/ppermute | solution.py:46
  54.1 3.5 %second.1 = (bf16[2,32,1536]{2,1,0:T(8,128)(2,1)S(1)}, bf16[2,32,1536]{2,1,0:T(8,128)(2,1)S(1)}, bf16[2,32,1536]{2,1,0:T(8,128)(2,1)S(1)}, bf16[2,32,1536]{2,1,0:T(8,128)(2,1)S(1)}) custom-call(bf16[32,4096]{1,0:T(8,128)(2,1)S(1)} %collective-permute-done.2.refs_0_, bf16[32,4096]{1,0:T(8,128)(2,1)S(1)} %collective-permute-done.4.refs_1_, ...), custom_call_target="tpu_custom_call" | custom-call | flops 3221225472 | bytes 15728640 | tf_op jit(solution)/shard_map/second/pallas_call | solution.py:20
  57.6 3.0 %collective-permute-start.18 = (bf16[2,32,1536]{2,1,0:T(8,128)(2,1)S(1)}, bf16[2,32,1536]{2,1,0:T(8,128)(2,1)S(1)}, u32[]{:S(2)}, u32[]{:S(2)}) collective-permute-start(bf16[2,32,1536]{2,1,0:T(8,128)(2,1)S(1)} %get-tuple-element.58), channel_id=1, source_target_pairs={{0,1},{1,2},{2,3},{3,0},{4,5},{5,6},{6,7},{7,4},{8,9},{9,10},{10,1... | collective-permute-start | bytes 589832 | tf_op jit(solution)/shard_map/ppermute | solution.py:46
  60.6 1.2 %collective-permute-start.19 = (bf16[2,32,1536]{2,1,0:T(8,128)(2,1)S(1)}, bf16[2,32,1536]{2,1,0:T(8,128)(2,1)S(1)}, u32[]{:S(2)}, u32[]{:S(2)}) collective-permute-start(bf16[2,32,1536]{2,1,0:T(8,128)(2,1)S(1)} %get-tuple-element.59), channel_id=1, source_target_pairs={{0,2},{1,3},{2,0},{3,1},{4,6},{5,7},{6,4},{7,5},{8,10},{9,11},{10,... | collective-permute-start | bytes 589832 | tf_op jit(solution)/shard_map/ppermute | solution.py:46
  62.4 4.6 %collective-permute-done.13.refs_3_ = bf16[2,32,1664]{2,1,0:T(8,128)(2,1)S(1)} collective-permute-done((bf16[2,32,1664]{2,1,0:T(8,128)(2,1)S(1)}, bf16[2,32,1664]{2,1,0:T(8,128)(2,1)S(1)}, u32[]{:S(2)}, u32[]{:S(2)}) %collective-permute-start.13) | collective-permute-done | bytes 213024 | tf_op jit(solution)/shard_map/ppermute | solution.py:46
  67.0 3.4 %collective-permute-done.18.refs_5_ = bf16[2,32,1536]{2,1,0:T(8,128)(2,1)S(1)} collective-permute-done((bf16[2,32,1536]{2,1,0:T(8,128)(2,1)S(1)}, bf16[2,32,1536]{2,1,0:T(8,128)(2,1)S(1)}, u32[]{:S(2)}, u32[]{:S(2)}) %collective-permute-start.18) | collective-permute-done | bytes 196640 | tf_op jit(solution)/shard_map/ppermute | solution.py:46
  70.4 0.8 collective-permute-done.19.refs_6_
  71.2 2.9 %collective-permute-done.20.refs_7_ = bf16[2,32,1536]{2,1,0:T(8,128)(2,1)S(1)} collective-permute-done((bf16[2,32,1536]{2,1,0:T(8,128)(2,1)S(1)}, bf16[2,32,1536]{2,1,0:T(8,128)(2,1)S(1)}, u32[]{:S(2)}, u32[]{:S(2)}) %collective-permute-start.20) | collective-permute-done | bytes 196640 | tf_op jit(solution)/shard_map/ppermute | solution.py:46
  74.4 2.6 %collective-permute-start.21 = (bf16[32,1664]{1,0:T(8,128)(2,1)S(1)}, bf16[32,1664]{1,0:T(8,128)(2,1)S(1)}, u32[]{:S(2)}, u32[]{:S(2)}) collective-permute-start(bf16[32,1664]{1,0:T(8,128)(2,1)S(1)} %get-tuple-element.62), channel_id=1, source_target_pairs={{0,4},{1,5},{2,6},{3,7},{4,8},{5,9},{6,10},{7,11},{8,12},{9,13},{1... | collective-permute-start | bytes 319496 | tf_op jit(solution)/shard_map/ppermute | solution.py:46
  77.0 2.9 %collective-permute-start.22 = (bf16[32,1664]{1,0:T(8,128)(2,1)S(1)}, bf16[32,1664]{1,0:T(8,128)(2,1)S(1)}, u32[]{:S(2)}, u32[]{:S(2)}) collective-permute-start(bf16[32,1664]{1,0:T(8,128)(2,1)S(1)} %get-tuple-element.63), channel_id=1, source_target_pairs={{0,8},{1,9},{2,10},{3,11},{4,12},{5,13},{6,14},{7,15},{8,0},{9,1},... | collective-permute-start | bytes 319496 | tf_op jit(solution)/shard_map/ppermute | solution.py:46
  79.9 2.5 %collective-permute-start.23 = (bf16[32,1664]{1,0:T(8,128)(2,1)S(1)}, bf16[32,1664]{1,0:T(8,128)(2,1)S(1)}, u32[]{:S(2)}, u32[]{:S(2)}) collective-permute-start(bf16[32,1664]{1,0:T(8,128)(2,1)S(1)} %get-tuple-element.64), channel_id=1, source_target_pairs={{0,12},{1,13},{2,14},{3,15},{4,0},{5,1},{6,2},{7,3},{8,4},{9,5},{1... | collective-permute-start | bytes 319496 | tf_op jit(solution)/shard_map/ppermute | solution.py:46
  82.4 4.3 %collective-permute-done.22.b = bf16[32,1664]{1,0:T(8,128)(2,1)S(1)} collective-permute-done((bf16[32,1664]{1,0:T(8,128)(2,1)S(1)}, bf16[32,1664]{1,0:T(8,128)(2,1)S(1)}, u32[]{:S(2)}, u32[]{:S(2)}) %collective-permute-start.22) | collective-permute-done | bytes 106528 | tf_op jit(solution)/shard_map/ppermute | solution.py:46
  86.7 4.4 %collective-permute-done.23.c = bf16[32,1664]{1,0:T(8,128)(2,1)S(1)} collective-permute-done((bf16[32,1664]{1,0:T(8,128)(2,1)S(1)}, bf16[32,1664]{1,0:T(8,128)(2,1)S(1)}, u32[]{:S(2)}, u32[]{:S(2)}) %collective-permute-start.23) | collective-permute-done | bytes 106528 | tf_op jit(solution)/shard_map/ppermute | solution.py:46
  91.1 0.8 finish.1
  (32 shorter events, 4.0 us)
Async XLA Ops:
  0.0 0.9 %copy-start = (bf16[1,2,16,4096]{3,2,1,0:T(8,128)(2,1)S(1)}, bf16[1,2,16,4096]{3,2,1,0:T(8,128)(2,1)}, u32[]{:S(2)}) copy-start(bf16[1,2,16,4096]{3,2,1,0:T(8,128)(2,1)} %param.4) | copy-start | bytes 786436
  2.1 22.0 %all-to-all-start = ((bf16[16,64,128]{2,1,0:T(8,128)(2,1)}), bf16[16,64,128]{2,1,0:T(8,128)(2,1)S(1)}, u32[]{:S(2)}, u32[]{:S(2)}) async-start(bf16[16,64,128]{2,1,0:T(8,128)(2,1)} %pack.1), calls=%async_computation | async-start | bytes 524288 | tf_op jit(solution)/shard_map/all_to_all | solution.py:362
  13.4 0.8 copy-start.1
  14.2 0.8 copy-start.2
  25.5 10.5 %collective-permute-start = (bf16[32,4096]{1,0:T(8,128)(2,1)S(1)}, bf16[32,4096]{1,0:T(8,128)(2,1)S(1)}, u32[]{:S(2)}, u32[]{:S(2)}) collective-permute-start(bf16[32,4096]{1,0:T(8,128)(2,1)S(1)} %ready.1.refs_0_), channel_id=1, source_target_pairs={{0,32},{1,33},{2,34},{3,35},{4,36},{5,37},{6,38},{7,39},{8,40},{9,... | collective-permute-start | bytes 786440 | tf_op jit(solution)/shard_map/ppermute | solution.py:46
  27.1 8.9 %collective-permute-start.1 = (bf16[32,4096]{1,0:T(8,128)(2,1)S(1)}, bf16[32,4096]{1,0:T(8,128)(2,1)S(1)}, u32[]{:S(2)}, u32[]{:S(2)}) collective-permute-start(bf16[32,4096]{1,0:T(8,128)(2,1)S(1)} %ready.1.refs_0_), channel_id=1, source_target_pairs={{0,96},{1,97},{2,98},{3,99},{4,100},{5,101},{6,102},{7,103},{8,104... | collective-permute-start | bytes 786440 | tf_op jit(solution)/shard_map/ppermute | solution.py:46
  28.8 10.1 %collective-permute-start.2 = (bf16[32,4096]{1,0:T(8,128)(2,1)S(1)}, bf16[32,4096]{1,0:T(8,128)(2,1)S(1)}, u32[]{:S(2)}, u32[]{:S(2)}) collective-permute-start(bf16[32,4096]{1,0:T(8,128)(2,1)S(1)} %ready.1.refs_0_), channel_id=1, source_target_pairs={{0,64},{1,65},{2,66},{3,67},{4,68},{5,69},{6,70},{7,71},{8,72},{9,... | collective-permute-start | bytes 786440 | tf_op jit(solution)/shard_map/ppermute | solution.py:46
  30.6 8.8 %collective-permute-start.3 = (bf16[32,4096]{1,0:T(8,128)(2,1)S(1)}, bf16[32,4096]{1,0:T(8,128)(2,1)S(1)}, u32[]{:S(2)}, u32[]{:S(2)}) collective-permute-start(bf16[32,4096]{1,0:T(8,128)(2,1)S(1)} %ready.1.refs_0_), channel_id=1, source_target_pairs={{0,128},{1,129},{2,130},{3,131},{4,132},{5,133},{6,134},{7,135},{8... | collective-permute-start | bytes 786440 | tf_op jit(solution)/shard_map/ppermute | solution.py:46
  31.5 8.8 %collective-permute-start.7 = (bf16[32,4096]{1,0:T(8,128)(2,1)S(1)}, bf16[32,4096]{1,0:T(8,128)(2,1)S(1)}, u32[]{:S(2)}, u32[]{:S(2)}) collective-permute-start(bf16[32,4096]{1,0:T(8,128)(2,1)S(1)} %ready.1.refs_0_), channel_id=1, source_target_pairs={{0,16},{1,17},{2,18},{3,19},{4,20},{5,21},{6,22},{7,23},{8,24},{9,... | collective-permute-start | bytes 786440 | tf_op jit(solution)/shard_map/ppermute | solution.py:46
  38.9 2.4 %collective-permute-start.8 = (bf16[32,4096]{1,0:T(8,128)(2,1)S(1)}, bf16[32,4096]{1,0:T(8,128)(2,1)S(1)}, u32[]{:S(2)}, u32[]{:S(2)}) collective-permute-start(bf16[32,4096]{1,0:T(8,128)(2,1)S(1)} %collective-permute-done.refs_1_), channel_id=1, source_target_pairs={{0,16},{1,17},{2,18},{3,19},{4,20},{5,21},{6,22},{7,23},{8,24},{9,... | collective-permute-start | bytes 786440 | tf_op jit(solution)/shard_map/ppermute | solution.py:46
  38.9 4.6 %collective-permute-start.9 = (bf16[32,4096]{1,0:T(8,128)(2,1)S(1)}, bf16[32,4096]{1,0:T(8,128)(2,1)S(1)}, u32[]{:S(2)}, u32[]{:S(2)}) collective-permute-start(bf16[32,4096]{1,0:T(8,128)(2,1)S(1)} %collective-permute-done.1.refs_2_), channel_id=1, source_target_pairs={{0,16},{1,17},{2,18},{3,19},{4,20},{5,21},{6,22},{7,23},{8,24},{9,... | collective-permute-start | bytes 786440 | tf_op jit(solution)/shard_map/ppermute | solution.py:46
  39.4 4.1 %collective-permute-start.10 = (bf16[32,4096]{1,0:T(8,128)(2,1)S(1)}, bf16[32,4096]{1,0:T(8,128)(2,1)S(1)}, u32[]{:S(2)}, u32[]{:S(2)}) collective-permute-start(bf16[32,4096]{1,0:T(8,128)(2,1)S(1)} %collective-permute-done.3.refs_3_), channel_id=1, source_target_pairs={{0,16},{1,17},{2,18},{3,19},{4,20},{5,21},{6,22},{7,23},{8,24},{9,... | collective-permute-start | bytes 786440 | tf_op jit(solution)/shard_map/ppermute | solution.py:46
  39.4 10.2 %collective-permute-start.6 = (bf16[32,4096]{1,0:T(8,128)(2,1)S(1)}, bf16[32,4096]{1,0:T(8,128)(2,1)S(1)}, u32[]{:S(2)}, u32[]{:S(2)}) collective-permute-start(bf16[32,4096]{1,0:T(8,128)(2,1)S(1)} %collective-permute-done.2.refs_0_), channel_id=1, source_target_pairs={{0,128},{1,129},{2,130},{3,131},{4,132},{5,133},{6,134},{7,135},{8... | collective-permute-start | bytes 786440 | tf_op jit(solution)/shard_map/ppermute | solution.py:46
  40.2 9.6 %collective-permute-start.4 = (bf16[32,4096]{1,0:T(8,128)(2,1)S(1)}, bf16[32,4096]{1,0:T(8,128)(2,1)S(1)}, u32[]{:S(2)}, u32[]{:S(2)}) collective-permute-start(bf16[32,4096]{1,0:T(8,128)(2,1)S(1)} %collective-permute-done.3.refs_3_), channel_id=1, source_target_pairs={{0,32},{1,33},{2,34},{3,35},{4,36},{5,37},{6,38},{7,39},{8,40},{9,... | collective-permute-start | bytes 786440 | tf_op jit(solution)/shard_map/ppermute | solution.py:46
  41.3 8.6 %collective-permute-start.5 = (bf16[32,4096]{1,0:T(8,128)(2,1)S(1)}, bf16[32,4096]{1,0:T(8,128)(2,1)S(1)}, u32[]{:S(2)}, u32[]{:S(2)}) collective-permute-start(bf16[32,4096]{1,0:T(8,128)(2,1)S(1)} %collective-permute-done.3.refs_3_), channel_id=1, source_target_pairs={{0,96},{1,97},{2,98},{3,99},{4,100},{5,101},{6,102},{7,103},{8,104... | collective-permute-start | bytes 786440 | tf_op jit(solution)/shard_map/ppermute | solution.py:46
  49.9 2.8 %collective-permute-start.14 = (bf16[32,4096]{1,0:T(8,128)(2,1)S(1)}, bf16[32,4096]{1,0:T(8,128)(2,1)S(1)}, u32[]{:S(2)}, u32[]{:S(2)}) collective-permute-start(bf16[32,4096]{1,0:T(8,128)(2,1)S(1)} %collective-permute-done.2.refs_0_), channel_id=1, source_target_pairs={{0,16},{1,17},{2,18},{3,19},{4,20},{5,21},{6,22},{7,23},{8,24},{9,... | collective-permute-start | bytes 786440 | tf_op jit(solution)/shard_map/ppermute | solution.py:46
  49.9 3.9 %collective-permute-start.15 = (bf16[32,4096]{1,0:T(8,128)(2,1)S(1)}, bf16[32,4096]{1,0:T(8,128)(2,1)S(1)}, u32[]{:S(2)}, u32[]{:S(2)}) collective-permute-start(bf16[32,4096]{1,0:T(8,128)(2,1)S(1)} %collective-permute-done.4.refs_1_), channel_id=1, source_target_pairs={{0,16},{1,17},{2,18},{3,19},{4,20},{5,21},{6,22},{7,23},{8,24},{9,... | collective-permute-start | bytes 786440 | tf_op jit(solution)/shard_map/ppermute | solution.py:46
  50.4 3.7 %collective-permute-start.16 = (bf16[32,4096]{1,0:T(8,128)(2,1)S(1)}, bf16[32,4096]{1,0:T(8,128)(2,1)S(1)}, u32[]{:S(2)}, u32[]{:S(2)}) collective-permute-start(bf16[32,4096]{1,0:T(8,128)(2,1)S(1)} %collective-permute-done.5.refs_2_), channel_id=1, source_target_pairs={{0,16},{1,17},{2,18},{3,19},{4,20},{5,21},{6,22},{7,23},{8,24},{9,... | collective-permute-start | bytes 786440 | tf_op jit(solution)/shard_map/ppermute | solution.py:46
  50.4 3.7 %collective-permute-start.17 = (bf16[32,4096]{1,0:T(8,128)(2,1)S(1)}, bf16[32,4096]{1,0:T(8,128)(2,1)S(1)}, u32[]{:S(2)}, u32[]{:S(2)}) collective-permute-start(bf16[32,4096]{1,0:T(8,128)(2,1)S(1)} %collective-permute-done.6.refs_3_), channel_id=1, source_target_pairs={{0,16},{1,17},{2,18},{3,19},{4,20},{5,21},{6,22},{7,23},{8,24},{9,... | collective-permute-start | bytes 786440 | tf_op jit(solution)/shard_map/ppermute | solution.py:46
  50.9 11.0 %collective-permute-start.11 = (bf16[2,32,1664]{2,1,0:T(8,128)(2,1)S(1)}, bf16[2,32,1664]{2,1,0:T(8,128)(2,1)S(1)}, u32[]{:S(2)}, u32[]{:S(2)}) collective-permute-start(bf16[2,32,1664]{2,1,0:T(8,128)(2,1)S(1)} %get-tuple-element.49), channel_id=1, source_target_pairs={{0,1},{1,2},{2,3},{3,0},{4,5},{5,6},{6,7},{7,4},{8,9},{9,10},{10,1... | collective-permute-start | bytes 638984 | tf_op jit(solution)/shard_map/ppermute | solution.py:46
  52.7 9.7 %collective-permute-start.12 = (bf16[2,32,1664]{2,1,0:T(8,128)(2,1)S(1)}, bf16[2,32,1664]{2,1,0:T(8,128)(2,1)S(1)}, u32[]{:S(2)}, u32[]{:S(2)}) collective-permute-start(bf16[2,32,1664]{2,1,0:T(8,128)(2,1)S(1)} %get-tuple-element.50), channel_id=1, source_target_pairs={{0,2},{1,3},{2,0},{3,1},{4,6},{5,7},{6,4},{7,5},{8,10},{9,11},{10,... | collective-permute-start | bytes 638984 | tf_op jit(solution)/shard_map/ppermute | solution.py:46
  53.8 13.2 %collective-permute-start.13 = (bf16[2,32,1664]{2,1,0:T(8,128)(2,1)S(1)}, bf16[2,32,1664]{2,1,0:T(8,128)(2,1)S(1)}, u32[]{:S(2)}, u32[]{:S(2)}) collective-permute-start(bf16[2,32,1664]{2,1,0:T(8,128)(2,1)S(1)} %get-tuple-element.51), channel_id=1, source_target_pairs={{0,3},{1,0},{2,1},{3,2},{4,7},{5,4},{6,5},{7,6},{8,11},{9,8},{10,9... | collective-permute-start | bytes 638984 | tf_op jit(solution)/shard_map/ppermute | solution.py:46
  57.6 12.8 %collective-permute-start.18 = (bf16[2,32,1536]{2,1,0:T(8,128)(2,1)S(1)}, bf16[2,32,1536]{2,1,0:T(8,128)(2,1)S(1)}, u32[]{:S(2)}, u32[]{:S(2)}) collective-permute-start(bf16[2,32,1536]{2,1,0:T(8,128)(2,1)S(1)} %get-tuple-element.58), channel_id=1, source_target_pairs={{0,1},{1,2},{2,3},{3,0},{4,5},{5,6},{6,7},{7,4},{8,9},{9,10},{10,1... | collective-permute-start | bytes 589832 | tf_op jit(solution)/shard_map/ppermute | solution.py:46
  60.6 10.6 %collective-permute-start.19 = (bf16[2,32,1536]{2,1,0:T(8,128)(2,1)S(1)}, bf16[2,32,1536]{2,1,0:T(8,128)(2,1)S(1)}, u32[]{:S(2)}, u32[]{:S(2)}) collective-permute-start(bf16[2,32,1536]{2,1,0:T(8,128)(2,1)S(1)} %get-tuple-element.59), channel_id=1, source_target_pairs={{0,2},{1,3},{2,0},{3,1},{4,6},{5,7},{6,4},{7,5},{8,10},{9,11},{10,... | collective-permute-start | bytes 589832 | tf_op jit(solution)/shard_map/ppermute | solution.py:46
  61.9 12.2 %collective-permute-start.20 = (bf16[2,32,1536]{2,1,0:T(8,128)(2,1)S(1)}, bf16[2,32,1536]{2,1,0:T(8,128)(2,1)S(1)}, u32[]{:S(2)}, u32[]{:S(2)}) collective-permute-start(bf16[2,32,1536]{2,1,0:T(8,128)(2,1)S(1)} %get-tuple-element.60), channel_id=1, source_target_pairs={{0,3},{1,0},{2,1},{3,2},{4,7},{5,4},{6,5},{7,6},{8,11},{9,8},{10,9... | collective-permute-start | bytes 589832 | tf_op jit(solution)/shard_map/ppermute | solution.py:46
  74.4 8.0 %collective-permute-start.21 = (bf16[32,1664]{1,0:T(8,128)(2,1)S(1)}, bf16[32,1664]{1,0:T(8,128)(2,1)S(1)}, u32[]{:S(2)}, u32[]{:S(2)}) collective-permute-start(bf16[32,1664]{1,0:T(8,128)(2,1)S(1)} %get-tuple-element.62), channel_id=1, source_target_pairs={{0,4},{1,5},{2,6},{3,7},{4,8},{5,9},{6,10},{7,11},{8,12},{9,13},{1... | collective-permute-start | bytes 319496 | tf_op jit(solution)/shard_map/ppermute | solution.py:46
  77.0 9.7 %collective-permute-start.22 = (bf16[32,1664]{1,0:T(8,128)(2,1)S(1)}, bf16[32,1664]{1,0:T(8,128)(2,1)S(1)}, u32[]{:S(2)}, u32[]{:S(2)}) collective-permute-start(bf16[32,1664]{1,0:T(8,128)(2,1)S(1)} %get-tuple-element.63), channel_id=1, source_target_pairs={{0,8},{1,9},{2,10},{3,11},{4,12},{5,13},{6,14},{7,15},{8,0},{9,1},... | collective-permute-start | bytes 319496 | tf_op jit(solution)/shard_map/ppermute | solution.py:46
  79.9 11.2 %collective-permute-start.23 = (bf16[32,1664]{1,0:T(8,128)(2,1)S(1)}, bf16[32,1664]{1,0:T(8,128)(2,1)S(1)}, u32[]{:S(2)}, u32[]{:S(2)}) collective-permute-start(bf16[32,1664]{1,0:T(8,128)(2,1)S(1)} %get-tuple-element.64), channel_id=1, source_target_pairs={{0,12},{1,13},{2,14},{3,15},{4,0},{5,1},{6,2},{7,3},{8,4},{9,5},{1... | collective-permute-start | bytes 319496 | tf_op jit(solution)/shard_map/ppermute | solution.py:46

commit v4 on v3

--- a/solution.py
+++ b/solution.py
@@ -47,23 +47,24 @@
 
 
 def pack_kernel(x_ref, out_ref, scratch):
-    for b in range(2):
-        for r in range(32):
-            piece = x_ref[b, :, r * 128 : (r + 1) * 128].astype(F32)
-            scratch[pl.ds(b * 32 + r, LAYERS, stride=64), :] = piece
-    out_ref[...] = scratch[...].astype(BF16).reshape(LAYERS, 64, 128)
+    for r in range(32):
+        piece = x_ref[0, :, r * 128 : (r + 1) * 128].astype(F32)
+        scratch[pl.ds(r, LAYERS, stride=32), :] = piece
+    out_ref[...] = scratch[...].astype(BF16).reshape(LAYERS, 32, 128)
 
 
 def pack(x):
-    return kernel_call(
+    return pl.pallas_call(
         pack_kernel,
-        "pack",
-        shape(LAYERS, 64, 128),
-        [x],
-        0,
-        2**19,
-        scratch_shapes=[pltpu.VMEM((LAYERS * 64, 128), F32)],
-    )
+        grid=(2,),
+        in_specs=[pl.BlockSpec((1, LAYERS, WIDTH), lambda b: (b, 0, 0))],
+        out_specs=pl.BlockSpec((LAYERS, 32, 128), lambda b: (0, b, 0)),
+        out_shape=shape(LAYERS, 64, 128),
+        scratch_shapes=[pltpu.VMEM((LAYERS * 32, 128), F32)],
+        compiler_params=pltpu.CompilerParams(vmem_limit_bytes=56 * MIB),
+        cost_estimate=pl.CostEstimate(flops=0, bytes_accessed=2**19, transcendentals=0),
+        name="pack",
+    )(x)
 
 
 def split(value, count):

time: 92.8 us -> 92.8 us (level)
  local copies, waits for them, and re-layouts: 2.46 us -> 1.51 us
    pallas_call x0 -> x1, Pallas kernels: none -> 2.05 us  [pack(): pl.pallas_call(pack_kernel, grid=(2,), in_specs=[pl.BlockSpec((1, LAYERS,...]
    pallas_call x6 -> x5, Pallas kernels: 7.45 us -> 6.29 us  [kernel_call(): pl.pallas_call(body, in_specs=[VMEM] * len(args), out_specs=VMEM if singl...]
    unnamed x6 -> x4, local copies, waits for them, and re-layouts: 2.46 us -> 1.51 us
where the time goes in v4:
time: 92.8 us; the launch traced here: 91.8 us
  starting transfers between devices  38.5 us (41%)
  waiting for transfers between devices  31.3 us (34%)
  Pallas kernels  20.4 us (22%)
  local copies, waits for them, and re-layouts  1.51 us (2%)
    ppermute x24, waiting for transfers between devices, shifted(): return lax.ppermute(value, ('dp', 'layer'), pairs)  28.4 us
    ppermute x24, starting transfers between devices, shifted(): return lax.ppermute(value, ('dp', 'layer'), pairs)  27.2 us
    pallas_call x2, Pallas kernels, corpus_call(): pl.pallas_call(body, in_specs=[VMEM] * (len(args) - 1) + [pl.BlockSpec(me...  12 us
    all_to_all x1, starting transfers between devices, per_device(): owned = lax.all_to_all(pack(query_grads[0]), 'layer', 0, 0, tiled=True)  11.3 us
    pallas_call x5, Pallas kernels, kernel_call(): pl.pallas_call(body, in_specs=[VMEM] * len(args), out_specs=VMEM if singl...  6.29 us
    all_to_all x1, waiting for transfers between devices, per_device(): owned = lax.all_to_all(pack(query_grads[0]), 'layer', 0, 0, tiled=True)  2.91 us
    pallas_call x1, Pallas kernels, pack(): pl.pallas_call(pack_kernel, grid=(2,), in_specs=[pl.BlockSpec((1, LAYERS,...  2.05 us
  transfers between devices with their start and end apart: 25, of which 11 were waited for; matrix products, arithmetic and copies ran while one was open for 0% of the time, Pallas kernels for 17%

profile of v4, /device:TPU:24, one launch (start us, length us, event | category | flops | bytes accessed | tf_op | source)
XLA Modules:
  0.0 91.8 jit_solution(13797015509760214756)
XLA Ops:
  0.0 2.1 %pack.1 = bf16[16,64,128]{2,1,0:T(8,128)(2,1)} custom-call(bf16[2,16,4096]{2,1,0:T(8,128)(2,1)} %bitcast.8), custom_call_target="tpu_custom_call" | custom-call | bytes 524288 | tf_op jit(solution)/shard_map/pack/pallas_call | solution.py:57
  2.1 11.3 %all-to-all-start = ((bf16[16,64,128]{2,1,0:T(8,128)(2,1)}), bf16[16,64,128]{2,1,0:T(8,128)(2,1)S(1)}, u32[]{:S(2)}, u32[]{:S(2)}) async-start(bf16[16,64,128]{2,1,0:T(8,128)(2,1)} %pack.1), calls=%async_computation | async-start | bytes 524288 | tf_op jit(solution)/shard_map/all_to_all | solution.py:363
  13.4 0.8 copy-done
  14.1 0.8 copy-done.1
  15.2 5.9 %power.1.refs_8_ = f32[12,128]{1,0:T(8,128)S(1)} custom-call(bf16[1536,4096]{1,0:T(8,128)(2,1)} %bitcast.6), custom_call_target="tpu_custom_call" | custom-call | flops 134217728 | bytes 13631488 | tf_op jit(solution)/shard_map/power/pallas_call | solution.py:195
  21.1 2.9 %all-to-all-done.x_ref = bf16[16,64,128]{2,1,0:T(8,128)(2,1)S(1)} async-done(((bf16[16,64,128]{2,1,0:T(8,128)(2,1)}), bf16[16,64,128]{2,1,0:T(8,128)(2,1)S(1)}, u32[]{:S(2)}, u32[]{:S(2)}) %all-to-all-start) | async-done | bytes 262176 | tf_op jit(solution)/shard_map/all_to_all | solution.py:363
  24.0 1.4 %ready.1.refs_0_ = bf16[32,4096]{1,0:T(8,128)(2,1)S(1)} custom-call(bf16[16,64,128]{2,1,0:T(8,128)(2,1)S(1)} %all-to-all-done.x_ref, bf16[64,256]{1,0:T(8,128)(2,1)S(1)} %get-tuple-element.38.left_ref, bf16[128,768]{1,0:T(8,128)(2,1)S(1)} %get-tuple-element.39.right_ref), custom_call_target="tpu_custom_call" | custom-call | flops 268435456 | bytes 524288 | tf_op jit(solution)/shard_map/ready/pallas_call | solution.py:20
  25.4 1.6 %collective-permute-start = (bf16[32,4096]{1,0:T(8,128)(2,1)S(1)}, bf16[32,4096]{1,0:T(8,128)(2,1)S(1)}, u32[]{:S(2)}, u32[]{:S(2)}) collective-permute-start(bf16[32,4096]{1,0:T(8,128)(2,1)S(1)} %ready.1.refs_0_), channel_id=1, source_target_pairs={{0,32},{1,33},{2,34},{3,35},{4,36},{5,37},{6,38},{7,39},{8,40},{9,... | collective-permute-start | bytes 786440 | tf_op jit(solution)/shard_map/ppermute | solution.py:46
  27.0 1.7 %collective-permute-start.1 = (bf16[32,4096]{1,0:T(8,128)(2,1)S(1)}, bf16[32,4096]{1,0:T(8,128)(2,1)S(1)}, u32[]{:S(2)}, u32[]{:S(2)}) collective-permute-start(bf16[32,4096]{1,0:T(8,128)(2,1)S(1)} %ready.1.refs_0_), channel_id=1, source_target_pairs={{0,96},{1,97},{2,98},{3,99},{4,100},{5,101},{6,102},{7,103},{8,104... | collective-permute-start | bytes 786440 | tf_op jit(solution)/shard_map/ppermute | solution.py:46
  28.8 1.8 %collective-permute-start.2 = (bf16[32,4096]{1,0:T(8,128)(2,1)S(1)}, bf16[32,4096]{1,0:T(8,128)(2,1)S(1)}, u32[]{:S(2)}, u32[]{:S(2)}) collective-permute-start(bf16[32,4096]{1,0:T(8,128)(2,1)S(1)} %ready.1.refs_0_), channel_id=1, source_target_pairs={{0,64},{1,65},{2,66},{3,67},{4,68},{5,69},{6,70},{7,71},{8,72},{9,... | collective-permute-start | bytes 786440 | tf_op jit(solution)/shard_map/ppermute | solution.py:46
  30.6 0.8 collective-permute-start.3
  31.4 4.5 %collective-permute-done.refs_1_ = bf16[32,4096]{1,0:T(8,128)(2,1)S(1)} collective-permute-done((bf16[32,4096]{1,0:T(8,128)(2,1)S(1)}, bf16[32,4096]{1,0:T(8,128)(2,1)S(1)}, u32[]{:S(2)}, u32[]{:S(2)}) %collective-permute-start) | collective-permute-done | bytes 262176 | tf_op jit(solution)/shard_map/ppermute | solution.py:46
  35.9 2.9 %collective-permute-done.2.refs_0_ = bf16[32,4096]{1,0:T(8,128)(2,1)S(1)} collective-permute-done((bf16[32,4096]{1,0:T(8,128)(2,1)S(1)}, bf16[32,4096]{1,0:T(8,128)(2,1)S(1)}, u32[]{:S(2)}, u32[]{:S(2)}) %collective-permute-start.2) | collective-permute-done | bytes 262176 | tf_op jit(solution)/shard_map/ppermute | solution.py:46
  39.3 0.8 collective-permute-start.6
  40.2 1.1 %collective-permute-start.4 = (bf16[32,4096]{1,0:T(8,128)(2,1)S(1)}, bf16[32,4096]{1,0:T(8,128)(2,1)S(1)}, u32[]{:S(2)}, u32[]{:S(2)}) collective-permute-start(bf16[32,4096]{1,0:T(8,128)(2,1)S(1)} %collective-permute-done.3.refs_3_), channel_id=1, source_target_pairs={{0,32},{1,33},{2,34},{3,35},{4,36},{5,37},{6,38},{7,39},{8,40},{9,... | collective-permute-start | bytes 786440 | tf_op jit(solution)/shard_map/ppermute | solution.py:46
  41.3 2.1 %collective-permute-start.5 = (bf16[32,4096]{1,0:T(8,128)(2,1)S(1)}, bf16[32,4096]{1,0:T(8,128)(2,1)S(1)}, u32[]{:S(2)}, u32[]{:S(2)}) collective-permute-start(bf16[32,4096]{1,0:T(8,128)(2,1)S(1)} %collective-permute-done.3.refs_3_), channel_id=1, source_target_pairs={{0,96},{1,97},{2,98},{3,99},{4,100},{5,101},{6,102},{7,103},{8,104... | collective-permute-start | bytes 786440 | tf_op jit(solution)/shard_map/ppermute | solution.py:46
  43.4 6.1 %first.1 = (bf16[2,32,1664]{2,1,0:T(8,128)(2,1)S(1)}, bf16[2,32,1664]{2,1,0:T(8,128)(2,1)S(1)}, bf16[2,32,1664]{2,1,0:T(8,128)(2,1)S(1)}, bf16[2,32,1664]{2,1,0:T(8,128)(2,1)S(1)}, bf16[1536,4096]{1,0:T(8,128)(2,1)S(1)}) custom-call(bf16[32,4096]{1,0:T(8,128)(2,1)S(1)} %ready.1.refs_0_, bf16[32,4096]{1,0:T(8,128)(2,1)S(1)} %collective-permute-done.refs_1_, ...), custom_call_target="tpu_custom_call" | custom-call | flops 3221225472 | bytes 13631488 | tf_op jit(solution)/shard_map/first/pallas_call | solution.py:195
  50.8 1.8 %collective-permute-start.11 = (bf16[2,32,1664]{2,1,0:T(8,128)(2,1)S(1)}, bf16[2,32,1664]{2,1,0:T(8,128)(2,1)S(1)}, u32[]{:S(2)}, u32[]{:S(2)}) collective-permute-start(bf16[2,32,1664]{2,1,0:T(8,128)(2,1)S(1)} %get-tuple-element.49), channel_id=1, source_target_pairs={{0,1},{1,2},{2,3},{3,0},{4,5},{5,6},{6,7},{7,4},{8,9},{9,10},{10,1... | collective-permute-start | bytes 638984 | tf_op jit(solution)/shard_map/ppermute | solution.py:46
  52.6 1.1 %collective-permute-start.12 = (bf16[2,32,1664]{2,1,0:T(8,128)(2,1)S(1)}, bf16[2,32,1664]{2,1,0:T(8,128)(2,1)S(1)}, u32[]{:S(2)}, u32[]{:S(2)}) collective-permute-start(bf16[2,32,1664]{2,1,0:T(8,128)(2,1)S(1)} %get-tuple-element.50), channel_id=1, source_target_pairs={{0,2},{1,3},{2,0},{3,1},{4,6},{5,7},{6,4},{7,5},{8,10},{9,11},{10,... | collective-permute-start | bytes 638984 | tf_op jit(solution)/shard_map/ppermute | solution.py:46
  54.0 3.5 %second.1 = (bf16[2,32,1536]{2,1,0:T(8,128)(2,1)S(1)}, bf16[2,32,1536]{2,1,0:T(8,128)(2,1)S(1)}, bf16[2,32,1536]{2,1,0:T(8,128)(2,1)S(1)}, bf16[2,32,1536]{2,1,0:T(8,128)(2,1)S(1)}) custom-call(bf16[32,4096]{1,0:T(8,128)(2,1)S(1)} %collective-permute-done.2.refs_0_, bf16[32,4096]{1,0:T(8,128)(2,1)S(1)} %collective-permute-done.4.refs_1_, ...), custom_call_target="tpu_custom_call" | custom-call | flops 3221225472 | bytes 15728640 | tf_op jit(solution)/shard_map/second/pallas_call | solution.py:20
  57.5 3.0 %collective-permute-start.18 = (bf16[2,32,1536]{2,1,0:T(8,128)(2,1)S(1)}, bf16[2,32,1536]{2,1,0:T(8,128)(2,1)S(1)}, u32[]{:S(2)}, u32[]{:S(2)}) collective-permute-start(bf16[2,32,1536]{2,1,0:T(8,128)(2,1)S(1)} %get-tuple-element.58), channel_id=1, source_target_pairs={{0,1},{1,2},{2,3},{3,0},{4,5},{5,6},{6,7},{7,4},{8,9},{9,10},{10,1... | collective-permute-start | bytes 589832 | tf_op jit(solution)/shard_map/ppermute | solution.py:46
  60.6 1.2 %collective-permute-start.19 = (bf16[2,32,1536]{2,1,0:T(8,128)(2,1)S(1)}, bf16[2,32,1536]{2,1,0:T(8,128)(2,1)S(1)}, u32[]{:S(2)}, u32[]{:S(2)}) collective-permute-start(bf16[2,32,1536]{2,1,0:T(8,128)(2,1)S(1)} %get-tuple-element.59), channel_id=1, source_target_pairs={{0,2},{1,3},{2,0},{3,1},{4,6},{5,7},{6,4},{7,5},{8,10},{9,11},{10,... | collective-permute-start | bytes 589832 | tf_op jit(solution)/shard_map/ppermute | solution.py:46
  62.3 4.6 %collective-permute-done.13.refs_3_ = bf16[2,32,1664]{2,1,0:T(8,128)(2,1)S(1)} collective-permute-done((bf16[2,32,1664]{2,1,0:T(8,128)(2,1)S(1)}, bf16[2,32,1664]{2,1,0:T(8,128)(2,1)S(1)}, u32[]{:S(2)}, u32[]{:S(2)}) %collective-permute-start.13) | collective-permute-done | bytes 213024 | tf_op jit(solution)/shard_map/ppermute | solution.py:46
  67.0 3.4 %collective-permute-done.18.refs_5_ = bf16[2,32,1536]{2,1,0:T(8,128)(2,1)S(1)} collective-permute-done((bf16[2,32,1536]{2,1,0:T(8,128)(2,1)S(1)}, bf16[2,32,1536]{2,1,0:T(8,128)(2,1)S(1)}, u32[]{:S(2)}, u32[]{:S(2)}) %collective-permute-start.18) | collective-permute-done | bytes 196640 | tf_op jit(solution)/shard_map/ppermute | solution.py:46
  70.4 0.8 collective-permute-done.19.refs_6_
  71.2 2.9 %collective-permute-done.20.refs_7_ = bf16[2,32,1536]{2,1,0:T(8,128)(2,1)S(1)} collective-permute-done((bf16[2,32,1536]{2,1,0:T(8,128)(2,1)S(1)}, bf16[2,32,1536]{2,1,0:T(8,128)(2,1)S(1)}, u32[]{:S(2)}, u32[]{:S(2)}) %collective-permute-start.20) | collective-permute-done | bytes 196640 | tf_op jit(solution)/shard_map/ppermute | solution.py:46
  74.4 2.6 %collective-permute-start.21 = (bf16[32,1664]{1,0:T(8,128)(2,1)S(1)}, bf16[32,1664]{1,0:T(8,128)(2,1)S(1)}, u32[]{:S(2)}, u32[]{:S(2)}) collective-permute-start(bf16[32,1664]{1,0:T(8,128)(2,1)S(1)} %get-tuple-element.62), channel_id=1, source_target_pairs={{0,4},{1,5},{2,6},{3,7},{4,8},{5,9},{6,10},{7,11},{8,12},{9,13},{1... | collective-permute-start | bytes 319496 | tf_op jit(solution)/shard_map/ppermute | solution.py:46
  76.9 2.9 %collective-permute-start.22 = (bf16[32,1664]{1,0:T(8,128)(2,1)S(1)}, bf16[32,1664]{1,0:T(8,128)(2,1)S(1)}, u32[]{:S(2)}, u32[]{:S(2)}) collective-permute-start(bf16[32,1664]{1,0:T(8,128)(2,1)S(1)} %get-tuple-element.63), channel_id=1, source_target_pairs={{0,8},{1,9},{2,10},{3,11},{4,12},{5,13},{6,14},{7,15},{8,0},{9,1},... | collective-permute-start | bytes 319496 | tf_op jit(solution)/shard_map/ppermute | solution.py:46
  79.8 2.5 %collective-permute-start.23 = (bf16[32,1664]{1,0:T(8,128)(2,1)S(1)}, bf16[32,1664]{1,0:T(8,128)(2,1)S(1)}, u32[]{:S(2)}, u32[]{:S(2)}) collective-permute-start(bf16[32,1664]{1,0:T(8,128)(2,1)S(1)} %get-tuple-element.64), channel_id=1, source_target_pairs={{0,12},{1,13},{2,14},{3,15},{4,0},{5,1},{6,2},{7,3},{8,4},{9,5},{1... | collective-permute-start | bytes 319496 | tf_op jit(solution)/shard_map/ppermute | solution.py:46
  82.4 4.3 %collective-permute-done.22.b = bf16[32,1664]{1,0:T(8,128)(2,1)S(1)} collective-permute-done((bf16[32,1664]{1,0:T(8,128)(2,1)S(1)}, bf16[32,1664]{1,0:T(8,128)(2,1)S(1)}, u32[]{:S(2)}, u32[]{:S(2)}) %collective-permute-start.22) | collective-permute-done | bytes 106528 | tf_op jit(solution)/shard_map/ppermute | solution.py:46
  86.6 4.4 %collective-permute-done.23.c = bf16[32,1664]{1,0:T(8,128)(2,1)S(1)} collective-permute-done((bf16[32,1664]{1,0:T(8,128)(2,1)S(1)}, bf16[32,1664]{1,0:T(8,128)(2,1)S(1)}, u32[]{:S(2)}, u32[]{:S(2)}) %collective-permute-start.23) | collective-permute-done | bytes 106528 | tf_op jit(solution)/shard_map/ppermute | solution.py:46
  91.0 0.8 finish.1
  (30 shorter events, 3.3 us)
Async XLA Ops:
  2.1 22.0 %all-to-all-start = ((bf16[16,64,128]{2,1,0:T(8,128)(2,1)}), bf16[16,64,128]{2,1,0:T(8,128)(2,1)S(1)}, u32[]{:S(2)}, u32[]{:S(2)}) async-start(bf16[16,64,128]{2,1,0:T(8,128)(2,1)} %pack.1), calls=%async_computation | async-start | bytes 524288 | tf_op jit(solution)/shard_map/all_to_all | solution.py:363
  13.4 0.8 copy-start
  14.1 0.8 copy-start.1
  25.4 10.5 %collective-permute-start = (bf16[32,4096]{1,0:T(8,128)(2,1)S(1)}, bf16[32,4096]{1,0:T(8,128)(2,1)S(1)}, u32[]{:S(2)}, u32[]{:S(2)}) collective-permute-start(bf16[32,4096]{1,0:T(8,128)(2,1)S(1)} %ready.1.refs_0_), channel_id=1, source_target_pairs={{0,32},{1,33},{2,34},{3,35},{4,36},{5,37},{6,38},{7,39},{8,40},{9,... | collective-permute-start | bytes 786440 | tf_op jit(solution)/shard_map/ppermute | solution.py:46
  27.0 8.9 %collective-permute-start.1 = (bf16[32,4096]{1,0:T(8,128)(2,1)S(1)}, bf16[32,4096]{1,0:T(8,128)(2,1)S(1)}, u32[]{:S(2)}, u32[]{:S(2)}) collective-permute-start(bf16[32,4096]{1,0:T(8,128)(2,1)S(1)} %ready.1.refs_0_), channel_id=1, source_target_pairs={{0,96},{1,97},{2,98},{3,99},{4,100},{5,101},{6,102},{7,103},{8,104... | collective-permute-start | bytes 786440 | tf_op jit(solution)/shard_map/ppermute | solution.py:46
  28.8 10.1 %collective-permute-start.2 = (bf16[32,4096]{1,0:T(8,128)(2,1)S(1)}, bf16[32,4096]{1,0:T(8,128)(2,1)S(1)}, u32[]{:S(2)}, u32[]{:S(2)}) collective-permute-start(bf16[32,4096]{1,0:T(8,128)(2,1)S(1)} %ready.1.refs_0_), channel_id=1, source_target_pairs={{0,64},{1,65},{2,66},{3,67},{4,68},{5,69},{6,70},{7,71},{8,72},{9,... | collective-permute-start | bytes 786440 | tf_op jit(solution)/shard_map/ppermute | solution.py:46
  30.6 8.8 %collective-permute-start.3 = (bf16[32,4096]{1,0:T(8,128)(2,1)S(1)}, bf16[32,4096]{1,0:T(8,128)(2,1)S(1)}, u32[]{:S(2)}, u32[]{:S(2)}) collective-permute-start(bf16[32,4096]{1,0:T(8,128)(2,1)S(1)} %ready.1.refs_0_), channel_id=1, source_target_pairs={{0,128},{1,129},{2,130},{3,131},{4,132},{5,133},{6,134},{7,135},{8... | collective-permute-start | bytes 786440 | tf_op jit(solution)/shard_map/ppermute | solution.py:46
  31.4 8.8 %collective-permute-start.7 = (bf16[32,4096]{1,0:T(8,128)(2,1)S(1)}, bf16[32,4096]{1,0:T(8,128)(2,1)S(1)}, u32[]{:S(2)}, u32[]{:S(2)}) collective-permute-start(bf16[32,4096]{1,0:T(8,128)(2,1)S(1)} %ready.1.refs_0_), channel_id=1, source_target_pairs={{0,16},{1,17},{2,18},{3,19},{4,20},{5,21},{6,22},{7,23},{8,24},{9,... | collective-permute-start | bytes 786440 | tf_op jit(solution)/shard_map/ppermute | solution.py:46
  38.8 2.4 %collective-permute-start.8 = (bf16[32,4096]{1,0:T(8,128)(2,1)S(1)}, bf16[32,4096]{1,0:T(8,128)(2,1)S(1)}, u32[]{:S(2)}, u32[]{:S(2)}) collective-permute-start(bf16[32,4096]{1,0:T(8,128)(2,1)S(1)} %collective-permute-done.refs_1_), channel_id=1, source_target_pairs={{0,16},{1,17},{2,18},{3,19},{4,20},{5,21},{6,22},{7,23},{8,24},{9,... | collective-permute-start | bytes 786440 | tf_op jit(solution)/shard_map/ppermute | solution.py:46
  38.8 4.6 %collective-permute-start.9 = (bf16[32,4096]{1,0:T(8,128)(2,1)S(1)}, bf16[32,4096]{1,0:T(8,128)(2,1)S(1)}, u32[]{:S(2)}, u32[]{:S(2)}) collective-permute-start(bf16[32,4096]{1,0:T(8,128)(2,1)S(1)} %collective-permute-done.1.refs_2_), channel_id=1, source_target_pairs={{0,16},{1,17},{2,18},{3,19},{4,20},{5,21},{6,22},{7,23},{8,24},{9,... | collective-permute-start | bytes 786440 | tf_op jit(solution)/shard_map/ppermute | solution.py:46
  39.3 4.1 %collective-permute-start.10 = (bf16[32,4096]{1,0:T(8,128)(2,1)S(1)}, bf16[32,4096]{1,0:T(8,128)(2,1)S(1)}, u32[]{:S(2)}, u32[]{:S(2)}) collective-permute-start(bf16[32,4096]{1,0:T(8,128)(2,1)S(1)} %collective-permute-done.3.refs_3_), channel_id=1, source_target_pairs={{0,16},{1,17},{2,18},{3,19},{4,20},{5,21},{6,22},{7,23},{8,24},{9,... | collective-permute-start | bytes 786440 | tf_op jit(solution)/shard_map/ppermute | solution.py:46
  39.3 10.2 %collective-permute-start.6 = (bf16[32,4096]{1,0:T(8,128)(2,1)S(1)}, bf16[32,4096]{1,0:T(8,128)(2,1)S(1)}, u32[]{:S(2)}, u32[]{:S(2)}) collective-permute-start(bf16[32,4096]{1,0:T(8,128)(2,1)S(1)} %collective-permute-done.2.refs_0_), channel_id=1, source_target_pairs={{0,128},{1,129},{2,130},{3,131},{4,132},{5,133},{6,134},{7,135},{8... | collective-permute-start | bytes 786440 | tf_op jit(solution)/shard_map/ppermute | solution.py:46
  40.2 9.6 %collective-permute-start.4 = (bf16[32,4096]{1,0:T(8,128)(2,1)S(1)}, bf16[32,4096]{1,0:T(8,128)(2,1)S(1)}, u32[]{:S(2)}, u32[]{:S(2)}) collective-permute-start(bf16[32,4096]{1,0:T(8,128)(2,1)S(1)} %collective-permute-done.3.refs_3_), channel_id=1, source_target_pairs={{0,32},{1,33},{2,34},{3,35},{4,36},{5,37},{6,38},{7,39},{8,40},{9,... | collective-permute-start | bytes 786440 | tf_op jit(solution)/shard_map/ppermute | solution.py:46
  41.3 8.6 %collective-permute-start.5 = (bf16[32,4096]{1,0:T(8,128)(2,1)S(1)}, bf16[32,4096]{1,0:T(8,128)(2,1)S(1)}, u32[]{:S(2)}, u32[]{:S(2)}) collective-permute-start(bf16[32,4096]{1,0:T(8,128)(2,1)S(1)} %collective-permute-done.3.refs_3_), channel_id=1, source_target_pairs={{0,96},{1,97},{2,98},{3,99},{4,100},{5,101},{6,102},{7,103},{8,104... | collective-permute-start | bytes 786440 | tf_op jit(solution)/shard_map/ppermute | solution.py:46
  49.8 2.8 %collective-permute-start.14 = (bf16[32,4096]{1,0:T(8,128)(2,1)S(1)}, bf16[32,4096]{1,0:T(8,128)(2,1)S(1)}, u32[]{:S(2)}, u32[]{:S(2)}) collective-permute-start(bf16[32,4096]{1,0:T(8,128)(2,1)S(1)} %collective-permute-done.2.refs_0_), channel_id=1, source_target_pairs={{0,16},{1,17},{2,18},{3,19},{4,20},{5,21},{6,22},{7,23},{8,24},{9,... | collective-permute-start | bytes 786440 | tf_op jit(solution)/shard_map/ppermute | solution.py:46
  49.8 3.9 %collective-permute-start.15 = (bf16[32,4096]{1,0:T(8,128)(2,1)S(1)}, bf16[32,4096]{1,0:T(8,128)(2,1)S(1)}, u32[]{:S(2)}, u32[]{:S(2)}) collective-permute-start(bf16[32,4096]{1,0:T(8,128)(2,1)S(1)} %collective-permute-done.4.refs_1_), channel_id=1, source_target_pairs={{0,16},{1,17},{2,18},{3,19},{4,20},{5,21},{6,22},{7,23},{8,24},{9,... | collective-permute-start | bytes 786440 | tf_op jit(solution)/shard_map/ppermute | solution.py:46
  50.3 3.7 %collective-permute-start.16 = (bf16[32,4096]{1,0:T(8,128)(2,1)S(1)}, bf16[32,4096]{1,0:T(8,128)(2,1)S(1)}, u32[]{:S(2)}, u32[]{:S(2)}) collective-permute-start(bf16[32,4096]{1,0:T(8,128)(2,1)S(1)} %collective-permute-done.5.refs_2_), channel_id=1, source_target_pairs={{0,16},{1,17},{2,18},{3,19},{4,20},{5,21},{6,22},{7,23},{8,24},{9,... | collective-permute-start | bytes 786440 | tf_op jit(solution)/shard_map/ppermute | solution.py:46
  50.3 3.7 %collective-permute-start.17 = (bf16[32,4096]{1,0:T(8,128)(2,1)S(1)}, bf16[32,4096]{1,0:T(8,128)(2,1)S(1)}, u32[]{:S(2)}, u32[]{:S(2)}) collective-permute-start(bf16[32,4096]{1,0:T(8,128)(2,1)S(1)} %collective-permute-done.6.refs_3_), channel_id=1, source_target_pairs={{0,16},{1,17},{2,18},{3,19},{4,20},{5,21},{6,22},{7,23},{8,24},{9,... | collective-permute-start | bytes 786440 | tf_op jit(solution)/shard_map/ppermute | solution.py:46
  50.8 11.0 %collective-permute-start.11 = (bf16[2,32,1664]{2,1,0:T(8,128)(2,1)S(1)}, bf16[2,32,1664]{2,1,0:T(8,128)(2,1)S(1)}, u32[]{:S(2)}, u32[]{:S(2)}) collective-permute-start(bf16[2,32,1664]{2,1,0:T(8,128)(2,1)S(1)} %get-tuple-element.49), channel_id=1, source_target_pairs={{0,1},{1,2},{2,3},{3,0},{4,5},{5,6},{6,7},{7,4},{8,9},{9,10},{10,1... | collective-permute-start | bytes 638984 | tf_op jit(solution)/shard_map/ppermute | solution.py:46
  52.6 9.7 %collective-permute-start.12 = (bf16[2,32,1664]{2,1,0:T(8,128)(2,1)S(1)}, bf16[2,32,1664]{2,1,0:T(8,128)(2,1)S(1)}, u32[]{:S(2)}, u32[]{:S(2)}) collective-permute-start(bf16[2,32,1664]{2,1,0:T(8,128)(2,1)S(1)} %get-tuple-element.50), channel_id=1, source_target_pairs={{0,2},{1,3},{2,0},{3,1},{4,6},{5,7},{6,4},{7,5},{8,10},{9,11},{10,... | collective-permute-start | bytes 638984 | tf_op jit(solution)/shard_map/ppermute | solution.py:46
  53.7 13.2 %collective-permute-start.13 = (bf16[2,32,1664]{2,1,0:T(8,128)(2,1)S(1)}, bf16[2,32,1664]{2,1,0:T(8,128)(2,1)S(1)}, u32[]{:S(2)}, u32[]{:S(2)}) collective-permute-start(bf16[2,32,1664]{2,1,0:T(8,128)(2,1)S(1)} %get-tuple-element.51), channel_id=1, source_target_pairs={{0,3},{1,0},{2,1},{3,2},{4,7},{5,4},{6,5},{7,6},{8,11},{9,8},{10,9... | collective-permute-start | bytes 638984 | tf_op jit(solution)/shard_map/ppermute | solution.py:46
  57.5 12.8 %collective-permute-start.18 = (bf16[2,32,1536]{2,1,0:T(8,128)(2,1)S(1)}, bf16[2,32,1536]{2,1,0:T(8,128)(2,1)S(1)}, u32[]{:S(2)}, u32[]{:S(2)}) collective-permute-start(bf16[2,32,1536]{2,1,0:T(8,128)(2,1)S(1)} %get-tuple-element.58), channel_id=1, source_target_pairs={{0,1},{1,2},{2,3},{3,0},{4,5},{5,6},{6,7},{7,4},{8,9},{9,10},{10,1... | collective-permute-start | bytes 589832 | tf_op jit(solution)/shard_map/ppermute | solution.py:46
  60.6 10.6 %collective-permute-start.19 = (bf16[2,32,1536]{2,1,0:T(8,128)(2,1)S(1)}, bf16[2,32,1536]{2,1,0:T(8,128)(2,1)S(1)}, u32[]{:S(2)}, u32[]{:S(2)}) collective-permute-start(bf16[2,32,1536]{2,1,0:T(8,128)(2,1)S(1)} %get-tuple-element.59), channel_id=1, source_target_pairs={{0,2},{1,3},{2,0},{3,1},{4,6},{5,7},{6,4},{7,5},{8,10},{9,11},{10,... | collective-permute-start | bytes 589832 | tf_op jit(solution)/shard_map/ppermute | solution.py:46
  61.8 12.2 %collective-permute-start.20 = (bf16[2,32,1536]{2,1,0:T(8,128)(2,1)S(1)}, bf16[2,32,1536]{2,1,0:T(8,128)(2,1)S(1)}, u32[]{:S(2)}, u32[]{:S(2)}) collective-permute-start(bf16[2,32,1536]{2,1,0:T(8,128)(2,1)S(1)} %get-tuple-element.60), channel_id=1, source_target_pairs={{0,3},{1,0},{2,1},{3,2},{4,7},{5,4},{6,5},{7,6},{8,11},{9,8},{10,9... | collective-permute-start | bytes 589832 | tf_op jit(solution)/shard_map/ppermute | solution.py:46
  74.4 8.0 %collective-permute-start.21 = (bf16[32,1664]{1,0:T(8,128)(2,1)S(1)}, bf16[32,1664]{1,0:T(8,128)(2,1)S(1)}, u32[]{:S(2)}, u32[]{:S(2)}) collective-permute-start(bf16[32,1664]{1,0:T(8,128)(2,1)S(1)} %get-tuple-element.62), channel_id=1, source_target_pairs={{0,4},{1,5},{2,6},{3,7},{4,8},{5,9},{6,10},{7,11},{8,12},{9,13},{1... | collective-permute-start | bytes 319496 | tf_op jit(solution)/shard_map/ppermute | solution.py:46
  76.9 9.7 %collective-permute-start.22 = (bf16[32,1664]{1,0:T(8,128)(2,1)S(1)}, bf16[32,1664]{1,0:T(8,128)(2,1)S(1)}, u32[]{:S(2)}, u32[]{:S(2)}) collective-permute-start(bf16[32,1664]{1,0:T(8,128)(2,1)S(1)} %get-tuple-element.63), channel_id=1, source_target_pairs={{0,8},{1,9},{2,10},{3,11},{4,12},{5,13},{6,14},{7,15},{8,0},{9,1},... | collective-permute-start | bytes 319496 | tf_op jit(solution)/shard_map/ppermute | solution.py:46
  79.8 11.2 %collective-permute-start.23 = (bf16[32,1664]{1,0:T(8,128)(2,1)S(1)}, bf16[32,1664]{1,0:T(8,128)(2,1)S(1)}, u32[]{:S(2)}, u32[]{:S(2)}) collective-permute-start(bf16[32,1664]{1,0:T(8,128)(2,1)S(1)} %get-tuple-element.64), channel_id=1, source_target_pairs={{0,12},{1,13},{2,14},{3,15},{4,0},{5,1},{6,2},{7,3},{8,4},{9,5},{1... | collective-permute-start | bytes 319496 | tf_op jit(solution)/shard_map/ppermute | solution.py:46
